TPU v7x, 256 devices: a whole 4x4x8 slice. The times are simulated.
256 devices in a mesh: cuts: 2 (over core), state: 128 (over z, y, x).
Axes of the slice: x: 4, y: 4, z: 8, core: 2. Of those that a mesh axis runs over, the one named last changes fastest.
Arguments:
- initial_states: bfloat16 [512, 32, 48, 128], P(('cuts', 'state')), parts along dimension 0, may hold values from -36 to 36
- potential: float32 [32, 48, 128], replicated, may hold values from -1 to 0
- bounds: int32 [4], P('cuts'), parts along dimension 0, may hold values from -32 to 159, as said below
Outputs:
- orthonormal: float32 [512, 196608], P('cuts', 'state'), parts along dimension 0
There are 2 independent parts, one for each index of `cuts`. A program takes and returns all parts, laid end to end along the dimension named above; an argument that names none is the same for every part. Nothing has to cross between parts.
Inputs may be any that keep to these rules, and one draw needn't show every extreme that they name: `bounds`: the first entry lies in -32 to -17, inside the spectrum of H, and the second in 136 to 159, above it; the anchor -1.125 lies below the spectrum.
All inputs are finite; a program needn't handle non-finite values.
Results may differ from a plain program's by a relative error of at most 0.0003.
Values sent between devices are 32-bit elements; how exact they have to be, the bound alone decides.
A program may use at most 128 MiB of HBM per device.

v0:
```python
import math

import jax
import jax.numpy as jnp
from jax import lax
from jax.sharding import PartitionSpec as P

DEGREE = 16


STENCIL_NEAR = 4.0 / 3.0
STENCIL_FAR = -1.0 / 12.0
STENCIL_SELF = -5.0 / 2.0
ANCHOR_VALUE = -1.125


def partner_2(value, axis, apart):
    return lax.ppermute(value, axis, [(i, i ^ 1 << apart) for i in range(lax.axis_size(axis))])


def laplace_periodic(values, axis_dim):
    near_sum = jnp.roll(values, 1, axis_dim) + jnp.roll(values, -1, axis_dim)
    far_sum = jnp.roll(values, 2, axis_dim) + jnp.roll(values, -2, axis_dim)
    return STENCIL_NEAR * near_sum + STENCIL_FAR * far_sum


def laplace_walled(values):
    extent = values.shape[1]
    padded = jnp.pad(values, ((0, 0), (2, 2), (0, 0), (0, 0)))
    near_sum = padded[:, 1 : extent + 1] + padded[:, 3 : extent + 3]
    far_sum = padded[:, 0:extent] + padded[:, 4 : extent + 4]
    return STENCIL_NEAR * near_sum + STENCIL_FAR * far_sum


def apply_hamiltonian(values, potential):
    laplace = 3.0 * STENCIL_SELF * values + laplace_walled(values)
    laplace = laplace + laplace_periodic(values, 2) + laplace_periodic(values, 3)
    return -0.5 * laplace + potential[None] * values


def filter_states(states, potential, bounds):
    low_end = bounds[0].astype(jnp.float32) / 64.0
    high_end = bounds[1].astype(jnp.float32) / 16.0
    half_width = (high_end - low_end) / 2.0
    centre = (high_end + low_end) / 2.0
    sigma_now = half_width / (ANCHOR_VALUE - centre)
    tau_value = 2.0 / sigma_now
    current = (apply_hamiltonian(states, potential) - centre * states) * (sigma_now / half_width)

    def degree_step(degree, carried):
        previous, current, sigma_now = carried
        sigma_next = 1.0 / (tau_value - sigma_now)
        latest = (apply_hamiltonian(current, potential) - centre * current) * (
            2.0 * sigma_next / half_width
        )
        latest = latest - sigma_now * sigma_next * previous
        return (current, latest, sigma_next)

    carried = lax.fori_loop(1, DEGREE, degree_step, (states, current, sigma_now))
    return carried[1]


def outer_product(left, right):
    return lax.dot_general(
        left,
        right,
        (((1,), (1,)), ((), ())),
        precision=lax.Precision.HIGHEST,
        preferred_element_type=jnp.float32,
    )


def per_device(initial_states, potential, bounds):
    filtered = filter_states(initial_states.astype(jnp.float32), potential, bounds)
    points = filtered.shape[1] * filtered.shape[2] * filtered.shape[3]
    flat = filtered.reshape(filtered.shape[0], points)
    row_block = lax.all_to_all(flat, "state", split_axis=1, concat_axis=0, tiled=True)
    gram_local = outer_product(row_block, row_block)
    factor = jnp.linalg.cholesky(gram_local)
    levels = lax.axis_size("state").bit_length() - 1
    bit_order = list(range(levels))
    for bit_number in bit_order:
        partner = partner_2(factor, "state", bit_number)
        merged = outer_product(factor, factor) + outer_product(partner, partner)
        factor = jnp.linalg.cholesky(merged)
    solved = lax.linalg.triangular_solve(factor, row_block, left_side=True, lower=True)
    return solved * math.sqrt(points)


def solution(mesh):
    return jax.shard_map(
        per_device,
        mesh=mesh,
        in_specs=(P(("cuts", "state"), None, None, None), P(), P("cuts")),
        out_specs=P("cuts", "state"),
        check_vma=False,
    )
```

profile of v0, /device:TPU:8, one launch (start us, length us, event | category | flops | bytes accessed | tf_op | source)
XLA Modules:
  0.0 799.3 jit_solution(11979443869534272593)
XLA Ops:
  24.9 328.8 %while.17 = (s32[]{:T(128)}, f32[2,32,48,128]{3,2,1,0:T(8,128)S(1)}, f32[2,32,48,128]{3,2,1,0:T(8,128)S(1)}, f32[]{:T(128)}, f32[32,48,128]{2,1,0:T(8,128)}, /*i...) while((s32[]{:T(128)}, f32[2,32,48,128]{3,2,1,0:T(8,128)S(1)}, ...), condition=%wide.region_1.2_spmd, body=%wide.region_0.1_spmd.sunk | while | flops 13762567 | bytes 55836888 | solution.py:59
  38.2 8.4 %fusion.194 = f32[2,32,48,128]{3,2,1,0:T(8,128)S(1)} fusion(f32[2,32,48,128]{3,2,1,0:T(8,128)S(1)} %get-tuple-element.351, f32[2,32,47,128]{3,2,1,0:T(8,128)} %get-tuple-element.316, f32[2,32,1,128]{3,2,1,0:T(1,128)S(1)} %get-tuple-element.317, f32[2,32,1,128]{3,2,1,0:T(1,128)S(1)} %get-tuple-element.318, ...), kind=kLoop, calls=%fused_computation.14.clone.1 | loop fusion | flops 13762560 | bytes 18087948 | tf_op jit(solution)/shard_map/while/body/eval_jaxpr/sub | solution.py:56
  60.1 8.4 %fusion.194 = f32[2,32,48,128]{3,2,1,0:T(8,128)S(1)} fusion(f32[2,32,48,128]{3,2,1,0:T(8,128)S(1)} %get-tuple-element.351, f32[2,32,47,128]{3,2,1,0:T(8,128)} %get-tuple-element.316, f32[2,32,1,128]{3,2,1,0:T(1,128)S(1)} %get-tuple-element.317, f32[2,32,1,128]{3,2,1,0:T(1,128)S(1)} %get-tuple-element.318, ...), kind=kLoop, calls=%fused_computation.14.clone.1 | loop fusion | flops 13762560 | bytes 18087948 | tf_op jit(solution)/shard_map/while/body/eval_jaxpr/sub | solution.py:56
  82.0 8.4 %fusion.194 = f32[2,32,48,128]{3,2,1,0:T(8,128)S(1)} fusion(f32[2,32,48,128]{3,2,1,0:T(8,128)S(1)} %get-tuple-element.351, f32[2,32,47,128]{3,2,1,0:T(8,128)} %get-tuple-element.316, f32[2,32,1,128]{3,2,1,0:T(1,128)S(1)} %get-tuple-element.317, f32[2,32,1,128]{3,2,1,0:T(1,128)S(1)} %get-tuple-element.318, ...), kind=kLoop, calls=%fused_computation.14.clone.1 | loop fusion | flops 13762560 | bytes 18087948 | tf_op jit(solution)/shard_map/while/body/eval_jaxpr/sub | solution.py:56
  191.6 8.4 %fusion.194 = f32[2,32,48,128]{3,2,1,0:T(8,128)S(1)} fusion(f32[2,32,48,128]{3,2,1,0:T(8,128)S(1)} %get-tuple-element.351, f32[2,32,47,128]{3,2,1,0:T(8,128)} %get-tuple-element.316, f32[2,32,1,128]{3,2,1,0:T(1,128)S(1)} %get-tuple-element.317, f32[2,32,1,128]{3,2,1,0:T(1,128)S(1)} %get-tuple-element.318, ...), kind=kLoop, calls=%fused_computation.14.clone.1 | loop fusion | flops 13762560 | bytes 18087948 | tf_op jit(solution)/shard_map/while/body/eval_jaxpr/sub | solution.py:56
  355.1 56.9 %all_to_all.19 = f32[2,128,1536]{2,0,1:T(2,128)S(1)} all-to-all(f32[2,128,1536]{2,0,1:T(2,128)S(1)} %copy.26), channel_id=1, replica_groups=mesh['cuts'=2,'state'=128] {'state'}, dimensions={1} | all-to-all | bytes 3145728 | tf_op jit(solution)/shard_map/all_to_all | solution.py:77
  414.7 11.7 %cholesky.382 = f32[128,128]{1,0:T(8,128)S(1)} custom-call(f32[128,128]{1,0:T(8,128)S(1)} %cholesky.650), custom_call_target="Cholesky" | custom-call | tf_op jit(solution)/shard_map/jit(cholesky)/cholesky | solution.py:79
  426.5 9.8 %custom-call.19 = f32[1,128,128]{1,2,0:T(8,128)S(1)} custom-call(f32[1,128,128]{2,1,0:T(8,128)S(1)} %get-tuple-element.207), custom_call_target="InvertDiagBlocksLowerTriangular" | custom-call | tf_op jit(solution)/shard_map/jit(cholesky)/cholesky | solution.py:79
  436.8 12.1 %cholesky.399 = f32[128,128]{1,0:T(8,128)S(1)} custom-call(f32[128,128]{1,0:T(8,128)S(1)} %convolution_subtract_fusion.1), custom_call_target="Cholesky" | custom-call | tf_op jit(solution)/shard_map/jit(cholesky)/cholesky | solution.py:79
  458.1 11.7 %cholesky.416 = f32[128,128]{1,0:T(8,128)S(1)} custom-call(f32[128,128]{1,0:T(8,128)S(1)} %cholesky.653), custom_call_target="Cholesky" | custom-call | tf_op jit(solution)/shard_map/jit(cholesky)/cholesky | solution.py:85
  469.9 9.8 %custom-call.20 = f32[1,128,128]{1,2,0:T(8,128)S(1)} custom-call(f32[1,128,128]{2,1,0:T(8,128)S(1)} %get-tuple-element.203), custom_call_target="InvertDiagBlocksLowerTriangular" | custom-call | tf_op jit(solution)/shard_map/jit(cholesky)/cholesky | solution.py:85
  480.2 11.7 %cholesky.433 = f32[128,128]{1,0:T(8,128)S(1)} custom-call(f32[128,128]{1,0:T(8,128)S(1)} %slice_subtract_fusion.6), custom_call_target="Cholesky" | custom-call | tf_op jit(solution)/shard_map/jit(cholesky)/cholesky | solution.py:85
  503.4 11.7 %cholesky.450 = f32[128,128]{1,0:T(8,128)S(1)} custom-call(f32[128,128]{1,0:T(8,128)S(1)} %cholesky.656), custom_call_target="Cholesky" | custom-call | tf_op jit(solution)/shard_map/jit(cholesky)/cholesky | solution.py:85
  515.2 9.8 %custom-call.21 = f32[1,128,128]{1,2,0:T(8,128)S(1)} custom-call(f32[1,128,128]{2,1,0:T(8,128)S(1)} %get-tuple-element.199), custom_call_target="InvertDiagBlocksLowerTriangular" | custom-call | tf_op jit(solution)/shard_map/jit(cholesky)/cholesky | solution.py:85
  525.5 11.7 %cholesky.467 = f32[128,128]{1,0:T(8,128)S(1)} custom-call(f32[128,128]{1,0:T(8,128)S(1)} %slice_subtract_fusion.5), custom_call_target="Cholesky" | custom-call | tf_op jit(solution)/shard_map/jit(cholesky)/cholesky | solution.py:85
  547.3 11.7 %cholesky.484 = f32[128,128]{1,0:T(8,128)S(1)} custom-call(f32[128,128]{1,0:T(8,128)S(1)} %cholesky.659), custom_call_target="Cholesky" | custom-call | tf_op jit(solution)/shard_map/jit(cholesky)/cholesky | solution.py:85
  559.0 9.8 %custom-call.22 = f32[1,128,128]{1,2,0:T(8,128)S(1)} custom-call(f32[1,128,128]{2,1,0:T(8,128)S(1)} %get-tuple-element.195), custom_call_target="InvertDiagBlocksLowerTriangular" | custom-call | tf_op jit(solution)/shard_map/jit(cholesky)/cholesky | solution.py:85
  569.3 11.7 %cholesky.501 = f32[128,128]{1,0:T(8,128)S(1)} custom-call(f32[128,128]{1,0:T(8,128)S(1)} %slice_subtract_fusion.4), custom_call_target="Cholesky" | custom-call | tf_op jit(solution)/shard_map/jit(cholesky)/cholesky | solution.py:85
  592.8 11.7 %cholesky.518 = f32[128,128]{1,0:T(8,128)S(1)} custom-call(f32[128,128]{1,0:T(8,128)S(1)} %cholesky.662), custom_call_target="Cholesky" | custom-call | tf_op jit(solution)/shard_map/jit(cholesky)/cholesky | solution.py:85
  604.6 9.8 %custom-call.23 = f32[1,128,128]{1,2,0:T(8,128)S(1)} custom-call(f32[1,128,128]{2,1,0:T(8,128)S(1)} %get-tuple-element.191), custom_call_target="InvertDiagBlocksLowerTriangular" | custom-call | tf_op jit(solution)/shard_map/jit(cholesky)/cholesky | solution.py:85
  614.9 11.7 %cholesky.535 = f32[128,128]{1,0:T(8,128)S(1)} custom-call(f32[128,128]{1,0:T(8,128)S(1)} %slice_subtract_fusion.3), custom_call_target="Cholesky" | custom-call | tf_op jit(solution)/shard_map/jit(cholesky)/cholesky | solution.py:85
  636.6 11.7 %cholesky.552 = f32[128,128]{1,0:T(8,128)S(1)} custom-call(f32[128,128]{1,0:T(8,128)S(1)} %cholesky.665), custom_call_target="Cholesky" | custom-call | tf_op jit(solution)/shard_map/jit(cholesky)/cholesky | solution.py:85
  648.4 9.8 %custom-call.24 = f32[1,128,128]{1,2,0:T(8,128)S(1)} custom-call(f32[1,128,128]{2,1,0:T(8,128)S(1)} %get-tuple-element.187), custom_call_target="InvertDiagBlocksLowerTriangular" | custom-call | tf_op jit(solution)/shard_map/jit(cholesky)/cholesky | solution.py:85
  658.7 11.7 %cholesky.569 = f32[128,128]{1,0:T(8,128)S(1)} custom-call(f32[128,128]{1,0:T(8,128)S(1)} %slice_subtract_fusion.2), custom_call_target="Cholesky" | custom-call | tf_op jit(solution)/shard_map/jit(cholesky)/cholesky | solution.py:85
  674.4 9.1 %collective-permute-done.5 = f32[256,256]{1,0:T(8,128)S(1)} collective-permute-done((f32[256,256]{1,0:T(8,128)S(1)}, f32[256,256]{1,0:T(8,128)S(1)}, u32[]{:S(2)}, u32[]{:S(2)}) %collective-permute-start.5) | collective-permute-done | bytes 262176 | tf_op jit(solution)/shard_map/ppermute | solution.py:18
  684.1 11.7 %cholesky.586 = f32[128,128]{1,0:T(8,128)S(1)} custom-call(f32[128,128]{1,0:T(8,128)S(1)} %cholesky.668), custom_call_target="Cholesky" | custom-call | tf_op jit(solution)/shard_map/jit(cholesky)/cholesky | solution.py:85
  695.9 9.8 %custom-call.25 = f32[1,128,128]{1,2,0:T(8,128)S(1)} custom-call(f32[1,128,128]{2,1,0:T(8,128)S(1)} %get-tuple-element.183), custom_call_target="InvertDiagBlocksLowerTriangular" | custom-call | tf_op jit(solution)/shard_map/jit(cholesky)/cholesky | solution.py:85
  706.2 11.7 %cholesky.603 = f32[128,128]{1,0:T(8,128)S(1)} custom-call(f32[128,128]{1,0:T(8,128)S(1)} %slice_subtract_fusion.1), custom_call_target="Cholesky" | custom-call | tf_op jit(solution)/shard_map/jit(cholesky)/cholesky | solution.py:85
  734.8 11.7 %cholesky.620 = f32[128,128]{1,0:T(8,128)S(1)} custom-call(f32[128,128]{1,0:T(8,128)S(1)} %cholesky.671), custom_call_target="Cholesky" | custom-call | tf_op jit(solution)/shard_map/jit(cholesky)/cholesky | solution.py:85
  746.5 9.8 %custom-call.26 = f32[1,128,128]{1,2,0:T(8,128)S(1)} custom-call(f32[1,128,128]{2,1,0:T(8,128)S(1)} %get-tuple-element.179), custom_call_target="InvertDiagBlocksLowerTriangular" | custom-call | tf_op jit(solution)/shard_map/jit(cholesky)/cholesky | solution.py:85
  756.8 11.9 %cholesky.637 = f32[128,128]{1,0:T(8,128)S(1)} custom-call(f32[128,128]{1,0:T(8,128)S(1)} %slice_subtract_fusion), custom_call_target="Cholesky" | custom-call | tf_op jit(solution)/shard_map/jit(cholesky)/cholesky | solution.py:85
  775.6 19.7 %custom-call.11 = f32[2,128,128]{1,2,0:T(8,128)S(1)} custom-call(f32[2,128,128]{2,1,0:T(8,128)S(1)} %get-tuple-element.115), custom_call_target="InvertDiagBlocksLowerTriangular" | custom-call | tf_op jit(solution)/shard_map/triangular_solve | solution.py:86
  (339 shorter events, 402.5 us)
Async XLA Ops:
  2.7 3.5 copy-start
  24.9 1.2 copy-start.1
  46.8 1.2 copy-start.1
  68.7 1.2 copy-start.1
  90.6 1.2 copy-start.1
  112.6 1.2 copy-start.1
  134.5 1.2 copy-start.1
  156.4 1.2 copy-start.1
  178.3 1.2 copy-start.1
  200.2 1.2 copy-start.1
  222.1 1.2 copy-start.1
  244.1 1.2 copy-start.1
  266.0 1.2 copy-start.1
  287.9 1.2 copy-start.1
  309.8 1.2 copy-start.1
  331.7 1.2 copy-start.1
  451.0 6.5 collective-permute-start
  494.7 8.1 %collective-permute-start.1 = (f32[256,256]{1,0:T(8,128)S(1)}, f32[256,256]{1,0:T(8,128)S(1)}, u32[]{:S(2)}, u32[]{:S(2)}) collective-permute-start(f32[256,256]{1,0:T(8,128)S(1)} %select_select_fusion.6), channel_id=1, source_target_pairs={{0,2},{1,3},{2,0},{3,1},{4,6},{5,7},{6,4},{7,5},{8,10},{9,11},{10,... | collective-permute-start | bytes 786440 | tf_op jit(solution)/shard_map/ppermute | solution.py:18
  540.0 6.7 collective-permute-start.2
  583.8 8.4 %collective-permute-start.3 = (f32[256,256]{1,0:T(8,128)S(1)}, f32[256,256]{1,0:T(8,128)S(1)}, u32[]{:S(2)}, u32[]{:S(2)}) collective-permute-start(f32[256,256]{1,0:T(8,128)S(1)} %select_select_fusion.4), channel_id=1, source_target_pairs={{0,8},{1,9},{2,10},{3,11},{4,12},{5,13},{6,14},{7,15},{8,0},{9,1},... | collective-permute-start | bytes 786440 | tf_op jit(solution)/shard_map/ppermute | solution.py:18
  629.3 6.6 collective-permute-start.4
  673.1 10.4 %collective-permute-start.5 = (f32[256,256]{1,0:T(8,128)S(1)}, f32[256,256]{1,0:T(8,128)S(1)}, u32[]{:S(2)}, u32[]{:S(2)}) collective-permute-start(f32[256,256]{1,0:T(8,128)S(1)} %select_select_fusion.2), channel_id=1, source_target_pairs={{0,32},{1,33},{2,34},{3,35},{4,36},{5,37},{6,38},{7,39},{8,40},{9,... | collective-permute-start | bytes 786440 | tf_op jit(solution)/shard_map/ppermute | solution.py:18
  720.7 12.5 %collective-permute-start.6 = (f32[256,256]{1,0:T(8,128)S(1)}, f32[256,256]{1,0:T(8,128)}, u32[]{:S(2)}, u32[]{:S(2)}) collective-permute-start(f32[256,256]{1,0:T(8,128)S(1)} %select_select_fusion.1), channel_id=1, source_target_pairs={{0,64},{1,65},{2,66},{3,67},{4,68},{5,69},{6,70},{7,71},{8,72},{9,... | collective-permute-start | bytes 786440 | tf_op jit(solution)/shard_map/ppermute | solution.py:18
where the time goes:
time: 808 us; the launch traced here: 799 us
  other arithmetic  432 us (53%)
  local copies, waits for them, and re-layouts  225 us (28%)
  blocking collectives  56.9 us (7%)
  waiting for transfers between devices  47 us (6%)
  matrix products  14.5 us (2%)
  between operations  13.1 us (2%)
    another operation x49, other arithmetic, per_device(): factor = jnp.linalg.cholesky(merged)  243 us
    sub x15, other arithmetic, degree_step(): latest = latest - sigma_now * sigma_next * previous  125 us
    slice x64, local copies, waits for them, and re-layouts, laplace_periodic(): far_sum = jnp.roll(values, 2, axis_dim) + jnp.roll(values, -2, axis_dim)  101 us
    slice x64, local copies, waits for them, and re-layouts, laplace_periodic(): near_sum = jnp.roll(values, 1, axis_dim) + jnp.roll(values, -1, axis_dim)  93.5 us
    all_to_all x1, blocking collectives, per_device(): lax.all_to_all(flat, 'state', split_axis=1, concat_axis=0, tiled=True)  56.9 us
    ppermute x7, waiting for transfers between devices, partner_2(): lax.ppermute(value, axis, [(i, i ^ 1 << apart) for i in range(lax.axis_si...  47 us
    another operation x6, other arithmetic, per_device(): factor = jnp.linalg.cholesky(gram_local)  34.4 us
    while x60, local copies, waits for them, and re-layouts  20.2 us
  transfers between devices with their start and end apart: 7, of which 7 were waited for; matrix products, arithmetic and copies ran while one was open for 1% of the time, Pallas kernels for 0%

commit v1 on v0

v1 whole, which is shorter than its diff:
```python
import functools
import math

import jax
import jax.numpy as jnp
from jax import lax
from jax.experimental import pallas as pl
from jax.experimental.pallas import tpu as pltpu
from jax.sharding import PartitionSpec as P

DEGREE = 16
ANCHOR_VALUE = -1.125
XB = 8
GY = 128


def chebyshev_scalars(bounds_ref):
    low_end = jnp.full((8, GY), bounds_ref[0].astype(jnp.float32), jnp.float32) / 64.0
    high_end = jnp.full((8, GY), bounds_ref[1].astype(jnp.float32), jnp.float32) / 16.0
    half_width = (high_end - low_end) / 2.0
    centre = (high_end + low_end) / 2.0
    place = (ANCHOR_VALUE - centre) / half_width
    before, now = jnp.ones_like(place), place
    for _ in range(DEGREE - 1):
        before, now = now, 2.0 * place * now - before
    return half_width, centre, 1.0 / now


def circulant():
    row = lax.rem(lax.broadcasted_iota(jnp.int32, (2 * GY, GY), 0), GY)
    column = lax.broadcasted_iota(jnp.int32, (2 * GY, GY), 1)
    apart = lax.rem(row - column + GY, GY)
    near = jnp.where((apart == 1) | (apart == GY - 1), -16.0, 0.0)
    far = jnp.where((apart == 2) | (apart == GY - 2), 1.0, 0.0)
    return (near + far).astype(jnp.bfloat16)


def filter_step(source, target, diagonal, matrix, factor, scale):
    planes, rows = diagonal.shape[0], diagonal.shape[1]
    values = source[pl.ds(2, planes)].reshape(planes * rows * 8, GY)
    high = values.astype(jnp.bfloat16)
    low = (values - high.astype(jnp.float32)).astype(jnp.bfloat16)
    along_y = jnp.dot(
        jnp.concatenate([high, low], 1), matrix, preferred_element_type=jnp.float32
    ).reshape(planes, rows, 8, GY)
    for z in range(planes):
        here = [source[z + 2, r] for r in range(rows)]
        ring = (
            [pltpu.roll(here[r], 1, 0) for r in (rows - 2, rows - 1)]
            + here
            + [pltpu.roll(here[r], 7, 0) for r in (0, 1)]
        )
        for r in range(rows):
            near = (source[z + 1, r] + source[z + 3, r]) + (ring[r + 1] + ring[r + 3])
            far = (source[z, r] + source[z + 4, r]) + (ring[r] + ring[r + 4])
            total = far - 16.0 * near + diagonal[z, r] * here[r] + along_y[z, r]
            latest = factor * total - target[z + 2, r]
            if scale is not None:
                latest = latest * scale
            target[z + 2, r] = latest


def filter_kernel(bounds_ref, states_ref, potential_ref, out_ref, buffers, diagonal, plane):
    states, planes, width, _ = states_ref.shape
    rows = width // 8
    half_width, centre, last_scale = chebyshev_scalars(bounds_ref)
    shift = 3.75 - centre
    factor = 2.0 / (24.0 * half_width)
    zero = jnp.zeros((rows, 8, GY), jnp.float32)

    def load_potential(z, _):
        for r in range(rows):
            diagonal[z, r] = 24.0 * (potential_ref[z, pl.ds(r, 8, stride=rows), :] + shift)
        return 0

    lax.fori_loop(0, planes, load_potential, 0)
    for buffer in range(2):
        for z in (0, 1, planes + 2, planes + 3):
            buffers[buffer, z] = zero
    even, odd = buffers.at[0], buffers.at[1]
    matrix = circulant()

    def one_state(state, _):
        def load(z, _):
            plane[...] = states_ref[state, z].astype(jnp.float32)
            for r in range(rows):
                even[z + 2, r] = plane[pl.ds(r, 8, stride=rows), :]
            odd[z + 2] = zero
            return 0

        lax.fori_loop(0, planes, load, 0)

        def two_steps(pair, _):
            first = jnp.where(pair == 0, 0.5 * factor, factor)
            filter_step(even, odd, diagonal, matrix, first, None)
            last = jnp.where(pair == DEGREE // 2 - 1, last_scale, 1.0)
            filter_step(odd, even, diagonal, matrix, factor, last)
            return 0

        lax.fori_loop(0, DEGREE // 2, two_steps, 0)

        def store(z, _):
            for r in range(rows):
                out_ref[state, z, pl.ds(r, 8, stride=rows), :] = even[z + 2, r]
            return 0

        lax.fori_loop(0, planes, store, 0)
        return 0

    lax.fori_loop(0, states, one_state, 0)


def filter_states(states, potential, bounds):
    planes, width = states.shape[1:3]
    return pl.pallas_call(
        filter_kernel,
        out_shape=jax.ShapeDtypeStruct(states.shape, jnp.float32),
        in_specs=[
            pl.BlockSpec(memory_space=pltpu.SMEM),
            pl.BlockSpec(memory_space=pltpu.VMEM),
            pl.BlockSpec(memory_space=pltpu.VMEM),
        ],
        out_specs=pl.BlockSpec(memory_space=pltpu.VMEM),
        scratch_shapes=[
            pltpu.VMEM((2, planes + 4, width // 8, 8, GY), jnp.float32),
            pltpu.VMEM((planes, width // 8, 8, GY), jnp.float32),
            pltpu.VMEM((width, GY), jnp.float32),
        ],
        compiler_params=pltpu.CompilerParams(vmem_limit_bytes=40 << 20),
        name="chebyshev_filter",
    )(bounds, states, potential)


def per_device(initial_states, potential, bounds):
    filtered = filter_states(initial_states, potential, bounds)
    devices = lax.axis_size("state")
    points = filtered.shape[1] * filtered.shape[2] * filtered.shape[3]
    pieces = filtered.reshape(filtered.shape[0], devices, points // devices // GY, GY)
    gathered = lax.all_to_all(pieces, "state", split_axis=1, concat_axis=0, tiled=True)
    row_block = gathered.reshape(-1, points // devices)
    gram_local = lax.dot_general(
        row_block,
        row_block,
        (((1,), (1,)), ((), ())),
        precision=lax.Precision.HIGHEST,
        preferred_element_type=jnp.float32,
    )
    gram = lax.psum(gram_local, "state")
    factor = jnp.linalg.cholesky(gram)
    solved = lax.linalg.triangular_solve(factor, row_block, left_side=True, lower=True)
    return solved * math.sqrt(points)


def solution(mesh):
    return jax.shard_map(
        per_device,
        mesh=mesh,
        in_specs=(P(("cuts", "state"), None, None, None), P(), P("cuts")),
        out_specs=P("cuts", "state"),
        check_vma=False,
    )
```

time: 808 us -> 370 us (0.46); the launches traced: 799 us -> 370 us
  other arithmetic: 432 us -> 56.1 us
  local copies, waits for them, and re-layouts: 225 us -> 10.9 us
  waiting for transfers between devices: 47 us -> 248 us
  blocking collectives: 56.9 us -> 0 us
  Pallas kernels: 0 us -> 17.8 us
  matrix products: 14.5 us -> 6.19 us
    another operation x55 -> x6, other arithmetic: 277 us -> 34.1 us  [per_device(): factor = jnp.linalg.cholesky(gram)]
    psum x0 -> x1, waiting for transfers between devices: none -> 207 us  [per_device(): gram = lax.psum(gram_local, 'state')]
    slice x129 -> x0, local copies, waits for them, and re-layouts: 196 us -> none  [the longest x64 101 us: laplace_periodic(): far_sum = jnp.roll(values, 2, axis_dim) + jnp.roll(values, -2, axis_dim)]
    sub x15 -> x0, other arithmetic: 125 us -> none  [degree_step(): latest = latest - sigma_now * sigma_next * previous]
    all_to_all x1 -> x0, blocking collectives: 56.9 us -> none  [per_device(): lax.all_to_all(flat, 'state', split_axis=1, concat_axis=0, tiled=True)]
    ppermute x7 -> x0, waiting for transfers between devices: 47 us -> none  [partner_2(): lax.ppermute(value, axis, [(i, i ^ 1 << apart) for i in range(lax.axis_si...]
    all_to_all x0 -> x1, waiting for transfers between devices: none -> 41.5 us  [per_device(): lax.all_to_all(pieces, 'state', split_axis=1, concat_axis=0, tiled=True)]
    while x60 -> x0, local copies, waits for them, and re-layouts: 20.2 us -> none
  transfers between devices with their start and end apart: 7 -> 2, of which waited for: 7 -> 2; matrix products, arithmetic and copies ran while one was open for 1% -> 0% of each run, Pallas kernels for 0% -> 0%
where the time goes in v1:
time: 370 us
  waiting for transfers between devices  248 us (67%)
  other arithmetic  56.1 us (15%)
  Pallas kernels  17.8 us (5%)
  starting transfers between devices  15.6 us (4%)
  between operations  14.8 us (4%)
  local copies, waits for them, and re-layouts  10.9 us (3%)
  matrix products  6.19 us (2%)
    psum x1, waiting for transfers between devices, per_device(): gram = lax.psum(gram_local, 'state')  207 us
    all_to_all x1, waiting for transfers between devices, per_device(): lax.all_to_all(pieces, 'state', split_axis=1, concat_axis=0, tiled=True)  41.5 us
    another operation x6, other arithmetic, per_device(): factor = jnp.linalg.cholesky(gram)  34.1 us
    another operation x3, other arithmetic, per_device(): lax.linalg.triangular_solve(factor, row_block, left_side=True, lower=True)  19.7 us
    pallas_call x1, Pallas kernels, filter_states(): pl.pallas_call(filter_kernel, out_shape=jax.ShapeDtypeStruct(states.shape...  17.8 us
    all_to_all x1, starting transfers between devices, per_device(): lax.all_to_all(pieces, 'state', split_axis=1, concat_axis=0, tiled=True)  15.3 us
  transfers between devices with their start and end apart: 2, of which 2 were waited for; matrix products, arithmetic and copies ran while one was open for 0% of the time, Pallas kernels for 0%

profile of v1, /device:TPU:8, one launch (start us, length us, event | category | flops | bytes accessed | tf_op | source)
XLA Modules:
  0.0 369.8 jit_solution(7361699191278403166)
XLA Ops:
  6.5 1.1 copy-done
  7.7 1.1 copy-done.1
  8.8 0.7 copy-done.2
  9.5 17.8 %chebyshev_filter.1 = f32[2,32,48,128]{3,2,1,0:T(8,128)S(1)} custom-call(s32[2]{0:T(128)S(1)} %copy-done.2, bf16[2,32,48,128]{3,2,1,0:T(8,128)(2,1)S(1)} %copy-done, f32[32,48,128]{2,1,0:T(8,128)S(1)} %copy-done.1), custom_call_target="tpu_custom_call" | custom-call | tf_op jit(solution)/shard_map/chebyshev_filter/pallas_call | solution.py:115
  27.2 2.4 copy.6
  29.6 15.3 %all-to-all-start = ((f32[2,128,12,128]{3,0,2,1:T(2,128)}), f32[2,128,12,128]{3,0,2,1:T(2,128)S(1)}, u32[]{:S(2)}, u32[]{:S(2)}) async-start(f32[2,128,12,128]{3,0,2,1:T(2,128)} %bitcast), calls=%async_computation | async-start | bytes 3145728 | tf_op jit(solution)/shard_map/all_to_all | solution.py:139
  44.9 0.2 all-reduce.3.cloned.1.call-start
  45.2 41.5 %all-to-all-done = f32[2,128,12,128]{3,0,2,1:T(2,128)S(1)} async-done(((f32[2,128,12,128]{3,0,2,1:T(2,128)}), f32[2,128,12,128]{3,0,2,1:T(2,128)S(1)}, u32[]{:S(2)}, u32[]{:S(2)}) %all-to-all-start) | async-done | bytes 1572896 | tf_op jit(solution)/shard_map/all_to_all | solution.py:139
  86.7 0.3 copy.7
  87.0 2.9 fusion
  90.0 0.1 fusion.13
  90.1 0.1 copy.10
  90.2 0.1 copy.11
  90.4 206.9 %all-reduce.3.cloned.1.call-done = f32[256,256]{0,1:T(8,128)} async-done(((f32[256,256]{0,1:T(8,128)}), f32[256,256]{0,1:T(8,128)}) %all-reduce.3.cloned.1.call-update) | async-done | bytes 262160 | tf_op jit(solution)/shard_map/psum | solution.py:148
  297.3 1.1 copy.9
  298.4 1.0 fusion.6
  299.4 11.7 %cholesky.50 = f32[128,128]{1,0:T(8,128)S(1)} custom-call(f32[128,128]{1,0:T(8,128)S(1)} %cholesky.118), custom_call_target="Cholesky" | custom-call | tf_op jit(solution)/shard_map/jit(cholesky)/cholesky | solution.py:149
  311.1 9.8 %custom-call.14 = f32[1,128,128]{1,2,0:T(8,128)S(1)} custom-call(f32[1,128,128]{2,1,0:T(8,128)S(1)} %get-tuple-element.28), custom_call_target="InvertDiagBlocksLowerTriangular" | custom-call | tf_op jit(solution)/shard_map/jit(cholesky)/cholesky | solution.py:149
  321.0 0.2 constant_dynamic-update-slice_fusion.1
  321.2 0.3 convolution_subtract_fusion.1
  321.4 11.9 %cholesky.105 = f32[128,128]{1,0:T(8,128)S(1)} custom-call(f32[128,128]{1,0:T(8,128)S(1)} %convolution_subtract_fusion.1), custom_call_target="Cholesky" | custom-call | tf_op jit(solution)/shard_map/jit(cholesky)/cholesky | solution.py:149
  333.4 0.6 compare_reduce_fusion
  335.3 3.8 %while.1 = (s32[]{:T(128)}, f32[256,256]{1,0:T(8,128)S(1)}, s32[2,2]{1,0:T(2,128)S(1)}, f32[2,128,128]{2,1,0:T(8,128)S(1)}, s32[]{:T(128)}) while((s32[]{:T(128)}, f32[256,256]{1,0:T(8,128)S(1)}, s32[2,2]{1,0:T(2,128)S(1)}, f32[2,128,128]{2,1,0:T(8,128)S(1)}, s32[]{:T(128)}) %tuple.24), condition=%wide.while_cond, body=%wide.while_body.sunk | while | flops 2 | bytes 131181 | solution.py:150
  335.3 0.6 fusion.19
  335.9 1.3 bitcast_dynamic-update-slice_fusion.2
  337.2 0.6 fusion.19
  337.8 1.3 bitcast_dynamic-update-slice_fusion.2
  339.1 19.7 %custom-call.15 = f32[2,128,128]{1,2,0:T(8,128)S(1)} custom-call(f32[2,128,128]{2,1,0:T(8,128)S(1)} %get-tuple-element.12), custom_call_target="InvertDiagBlocksLowerTriangular" | custom-call | tf_op jit(solution)/shard_map/triangular_solve | solution.py:150
  358.8 1.0 fusion.3
  359.8 1.0 convolution_subtract_fusion
  360.8 0.8 fusion.8
  361.6 1.3 maximum_multiply_fusion
  (14 shorter events, 0.2 us)
Async XLA Ops:
  6.5 1.1 copy-start
  7.7 1.1 copy-start.1
  8.8 0.7 copy-start.2
  29.6 57.1 %all-to-all-start = ((f32[2,128,12,128]{3,0,2,1:T(2,128)}), f32[2,128,12,128]{3,0,2,1:T(2,128)S(1)}, u32[]{:S(2)}, u32[]{:S(2)}) async-start(f32[2,128,12,128]{3,0,2,1:T(2,128)} %bitcast), calls=%async_computation | async-start | bytes 3145728 | tf_op jit(solution)/shard_map/all_to_all | solution.py:139
  44.9 252.3 %all-reduce.3.cloned.1.call-start = ((), (), s32[]{:S(2)}) async-start(), calls=%async_computation.1 | async-start | bytes 524288 | tf_op jit(solution)/shard_map/psum | solution.py:148
Sparse Core Ops, SparseCore 0:
  90.1 207.1 all-reduce.2

commit v2 on v1

--- a/solution.py
+++ b/solution.py
@@ -60,9 +60,73 @@
             target[z + 2, r] = latest
 
 
-def filter_kernel(bounds_ref, states_ref, potential_ref, out_ref, buffers, diagonal, plane):
+PLANES_Z = 8
+PLANE_XY = 16
+
+
+def neighbour(me, number):
+    dz, dy, dx = lax.rem(number, 8), lax.rem(lax.div(number, 8), 4), lax.div(number, 32)
+    z, y, x = lax.div(me, 16), lax.rem(lax.div(me, 4), 4), lax.rem(me, 4)
+    return lax.rem(z + dz, 8) * 16 + lax.rem(y + dy, 4) * 4 + lax.rem(x + dx, 4)
+
+
+def remote(source, target, send, receive, peer):
+    return pltpu.make_async_remote_copy(
+        src_ref=source,
+        dst_ref=target,
+        send_sem=send,
+        recv_sem=receive,
+        device_id={"state": peer},
+        device_id_type=pl.DeviceIdType.MESH,
+    )
+
+
+def wait_bytes(ref, semaphore):
+    pltpu.make_async_copy(ref, ref, semaphore).wait()
+
+
+def filter_gram_kernel(
+    bounds_ref,
+    states_ref,
+    potential_ref,
+    rows_ref,
+    gram_ref,
+    buffers,
+    diagonal,
+    plane,
+    outbox,
+    inbox,
+    block,
+    partial,
+    in_plane,
+    in_column,
+    gathered,
+    send_sem,
+    recv_sem,
+    own_sem,
+    rows_sem,
+    sum_send,
+    sum_recv,
+):
     states, planes, width, _ = states_ref.shape
     rows = width // 8
+    devices = 128
+    piece = planes * width // devices
+    me = lax.axis_index("state")
+
+    barrier = pltpu.get_barrier_semaphore()
+
+    def greet(number, _):
+        pl.semaphore_signal(
+            barrier,
+            inc=1,
+            device_id={"state": neighbour(me, number)},
+            device_id_type=pl.DeviceIdType.MESH,
+        )
+        return 0
+
+    lax.fori_loop(1, devices, greet, 0)
+
     half_width, centre, last_scale = chebyshev_scalars(bounds_ref)
     shift = 3.75 - centre
     factor = 2.0 / (24.0 * half_width)
@@ -101,54 +165,182 @@
 
         def store(z, _):
             for r in range(rows):
-                out_ref[state, z, pl.ds(r, 8, stride=rows), :] = even[z + 2, r]
+                outbox[pl.ds(state * planes * width + z * width + r, 8, stride=rows), :] = even[z + 2, r]
             return 0
 
         lax.fori_loop(0, planes, store, 0)
+
+        @pl.when(state == 0)
+        def _():
+            pl.semaphore_wait(barrier, devices - 1)
+
+        def send(number, _):
+            peer = neighbour(me, number)
+            remote(
+                outbox.at[pl.ds((state * devices + peer) * piece, piece)],
+                inbox.at[pl.ds((me * states + state) * piece, piece)],
+                send_sem,
+                recv_sem,
+                peer,
+            ).start()
+            return 0
+
+        lax.fori_loop(1, devices, send, 0)
+        pltpu.make_async_copy(
+            outbox.at[pl.ds((state * devices + me) * piece, piece)],
+            inbox.at[pl.ds((me * states + state) * piece, piece)],
+            own_sem.at[state],
+        ).start()
         return 0
 
     lax.fori_loop(0, states, one_state, 0)
-
-
-def filter_states(states, potential, bounds):
-    planes, width = states.shape[1:3]
+    for state in range(states):
+        pltpu.make_async_copy(
+            outbox.at[pl.ds((state * devices + me) * piece, piece)],
+            inbox.at[pl.ds((me * states + state) * piece, piece)],
+            own_sem.at[state],
+        ).wait()
+    wait_bytes(inbox.at[pl.ds(0, (devices - 1) * states * piece)], recv_sem)
+    wait_bytes(outbox.at[pl.ds(0, (devices - 1) * states * piece)], send_sem)
+
+    total = devices * states
+
+    def gram_piece(column, _):
+        here = inbox[pl.ds(column, total, stride=piece), :]
+        block[:, pl.ds(pl.multiple_of(column * GY, GY), GY)] = here
+        return 0
+
+    lax.fori_loop(0, piece, gram_piece, 0)
+    rows_copy = pltpu.make_async_copy(block, rows_ref, rows_sem)
+    rows_copy.start()
+    half = total // 2
+
+    def product(left, right):
+        return lax.dot_general(
+            left,
+            right,
+            (((1,), (1,)), ((), ())),
+            precision=lax.Precision.HIGHEST,
+            preferred_element_type=jnp.float32,
+        )
+
+    partial[0:half] = product(block[0:half], block[0:half])
+    partial[half : 2 * half] = product(block[half:], block[0:half])
+    partial[2 * half : 3 * half] = product(block[half:], block[half:])
+
+    count = 3 * half // PLANE_XY
+    mine, level = lax.rem(me, PLANE_XY), lax.div(me, PLANE_XY)
+
+    def plane_peer(number):
+        y, x = lax.div(mine, 4), lax.rem(mine, 4)
+        return lax.rem(y + lax.div(number, 4), 4) * 4 + lax.rem(x + lax.rem(number, 4), 4)
+
+    def share(number, _):
+        to = plane_peer(number)
+        remote(
+            partial.at[pl.ds(pl.multiple_of(to * count, 8), count)],
+            in_plane.at[mine],
+            sum_send.at[0],
+            sum_recv.at[0],
+            level * PLANE_XY + to,
+        ).start()
+        return 0
+
+    lax.fori_loop(1, PLANE_XY, share, 0)
+    in_plane[mine] = partial[pl.ds(pl.multiple_of(mine * count, 8), count), :]
+    wait_bytes(in_plane.at[pl.ds(0, PLANE_XY - 1)], sum_recv.at[0])
+    summed = in_plane[0]
+    for number in range(1, PLANE_XY):
+        summed = summed + in_plane[number]
+    in_column[level] = summed
+
+    def along_z(number, _):
+        to = lax.rem(level + number, PLANES_Z)
+        remote(
+            in_column.at[level],
+            in_column.at[level],
+            sum_send.at[1],
+            sum_recv.at[1],
+            to * PLANE_XY + mine,
+        ).start()
+        return 0
+
+    lax.fori_loop(1, PLANES_Z, along_z, 0)
+    wait_bytes(in_column.at[pl.ds(0, PLANES_Z - 1)], sum_recv.at[1])
+    summed = in_column[0]
+    for number in range(1, PLANES_Z):
+        summed = summed + in_column[number]
+    here = pl.ds(pl.multiple_of(mine * count, 8), count)
+    gathered[here, :] = summed
+
+    def spread(number, _):
+        remote(
+            gathered.at[here],
+            gathered.at[here],
+            sum_send.at[2],
+            sum_recv.at[2],
+            level * PLANE_XY + plane_peer(number),
+        ).start()
+        return 0
+
+    lax.fori_loop(1, PLANE_XY, spread, 0)
+    wait_bytes(gathered.at[pl.ds(0, count * (PLANE_XY - 1))], sum_recv.at[2])
+    gram_ref[0:half, 0:half] = gathered[0:half]
+    gram_ref[half:, 0:half] = gathered[half : 2 * half]
+    gram_ref[0:half, half:] = gathered[half : 2 * half].T
+    gram_ref[half:, half:] = gathered[2 * half :]
+    wait_bytes(in_plane.at[pl.ds(0, PLANE_XY - 1)], sum_send.at[0])
+    wait_bytes(in_column.at[pl.ds(0, PLANES_Z - 1)], sum_send.at[1])
+    wait_bytes(gathered.at[pl.ds(0, count * (PLANE_XY - 1))], sum_send.at[2])
+    rows_copy.wait()
+
+
+def filter_and_gram(states, potential, bounds):
+    count, planes, width = states.shape[:3]
+    total = count * 128
+    points = planes * width * GY // 128
     return pl.pallas_call(
-        filter_kernel,
-        out_shape=jax.ShapeDtypeStruct(states.shape, jnp.float32),
+        filter_gram_kernel,
+        out_shape=[
+            jax.ShapeDtypeStruct((total, points), jnp.float32),
+            jax.ShapeDtypeStruct((total, total), jnp.float32),
+        ],
         in_specs=[
             pl.BlockSpec(memory_space=pltpu.SMEM),
             pl.BlockSpec(memory_space=pltpu.VMEM),
             pl.BlockSpec(memory_space=pltpu.VMEM),
         ],
-        out_specs=pl.BlockSpec(memory_space=pltpu.VMEM),
+        out_specs=[pl.BlockSpec(memory_space=pl.ANY), pl.BlockSpec(memory_space=pltpu.VMEM)],
         scratch_shapes=[
             pltpu.VMEM((2, planes + 4, width // 8, 8, GY), jnp.float32),
             pltpu.VMEM((planes, width // 8, 8, GY), jnp.float32),
             pltpu.VMEM((width, GY), jnp.float32),
+            pltpu.VMEM((count * planes * width, GY), jnp.float32),
+            pltpu.VMEM((count * planes * width, GY), jnp.float32),
+            pltpu.VMEM((total, points), jnp.float32),
+            pltpu.VMEM((total * 3 // 2, GY), jnp.float32),
+            pltpu.VMEM((PLANE_XY, total * 3 // 2 // PLANE_XY, GY), jnp.float32),
+            pltpu.VMEM((PLANES_Z, total * 3 // 2 // PLANE_XY, GY), jnp.float32),
+            pltpu.VMEM((total * 3 // 2, GY), jnp.float32),
+            pltpu.SemaphoreType.DMA,
+            pltpu.SemaphoreType.DMA,
+            pltpu.SemaphoreType.DMA((count,)),
+            pltpu.SemaphoreType.DMA,
+            pltpu.SemaphoreType.DMA((3,)),
+            pltpu.SemaphoreType.DMA((3,)),
         ],
-        compiler_params=pltpu.CompilerParams(vmem_limit_bytes=40 << 20),
-        name="chebyshev_filter",
+        compiler_params=pltpu.CompilerParams(
+            vmem_limit_bytes=40 << 20, collective_id=0, has_side_effects=True
+        ),
+        name="filter_and_gram",
     )(bounds, states, potential)
 
 
 def per_device(initial_states, potential, bounds):
-    filtered = filter_states(initial_states, potential, bounds)
-    devices = lax.axis_size("state")
-    points = filtered.shape[1] * filtered.shape[2] * filtered.shape[3]
-    pieces = filtered.reshape(filtered.shape[0], devices, points // devices // GY, GY)
-    gathered = lax.all_to_all(pieces, "state", split_axis=1, concat_axis=0, tiled=True)
-    row_block = gathered.reshape(-1, points // devices)
-    gram_local = lax.dot_general(
-        row_block,
-        row_block,
-        (((1,), (1,)), ((), ())),
-        precision=lax.Precision.HIGHEST,
-        preferred_element_type=jnp.float32,
-    )
-    gram = lax.psum(gram_local, "state")
+    row_block, gram = filter_and_gram(initial_states, potential, bounds)
     factor = jnp.linalg.cholesky(gram)
     solved = lax.linalg.triangular_solve(factor, row_block, left_side=True, lower=True)
-    return solved * math.sqrt(points)
+    return solved * math.sqrt(math.prod(initial_states.shape[1:]))
 
 
 def solution(mesh):

time: 370 us -> 142 us (0.38)
  waiting for transfers between devices: 248 us -> 0 us
  Pallas kernels: 17.8 us -> 74.8 us
  starting transfers between devices: 15.6 us -> 0 us
  between operations: 14.8 us -> 1.36 us
  local copies, waits for them, and re-layouts: 10.9 us -> 7.17 us
    psum x1 -> x0, waiting for transfers between devices: 207 us -> none  [per_device(): gram = lax.psum(gram_local, 'state')]
    pallas_call x1, Pallas kernels: 17.8 us -> 74.8 us  [filter_and_gram(): pl.pallas_call(filter_gram_kernel, out_shape=[jax.ShapeDtypeStruct((total...]
    all_to_all x1 -> x0, waiting for transfers between devices: 41.5 us -> none  [per_device(): lax.all_to_all(pieces, 'state', split_axis=1, concat_axis=0, tiled=True)]
    all_to_all x1 -> x0, starting transfers between devices: 15.3 us -> none  [per_device(): lax.all_to_all(pieces, 'state', split_axis=1, concat_axis=0, tiled=True)]
  transfers between devices with their start and end apart: 2 -> 0, of which waited for: 2 -> 0; matrix products, arithmetic and copies ran while one was open for 0% -> 0% of each run, Pallas kernels for 0% -> 0%
where the time goes in v2:
time: 142 us
  Pallas kernels  74.8 us (53%)
  other arithmetic  55.3 us (39%)
  local copies, waits for them, and re-layouts  7.17 us (5%)
  matrix products  2.93 us (2%)
    pallas_call x1, Pallas kernels, filter_and_gram(): pl.pallas_call(filter_gram_kernel, out_shape=[jax.ShapeDtypeStruct((total...  74.8 us
    another operation x6, other arithmetic, per_device(): factor = jnp.linalg.cholesky(gram)  34 us
    another operation x3, other arithmetic, per_device(): lax.linalg.triangular_solve(factor, row_block, left_side=True, lower=True)  19.9 us
    another operation x6, local copies, waits for them, and re-layouts  4.02 us
    unnamed x6, local copies, waits for them, and re-layouts  2.92 us

profile of v2, /device:TPU:8, one launch (start us, length us, event | category | flops | bytes accessed | tf_op | source)
XLA Modules:
  0.0 141.6 jit_solution(15182942530967838091)
XLA Ops:
  0.0 0.1 triangular_solve.57
  0.1 0.0 copy-start
  0.1 1.1 copy-done
  1.2 0.0 copy-start.1
  1.2 1.1 copy-done.1
  2.3 0.0 copy-start.2
  2.3 0.7 copy-done.2
  3.0 74.8 %filter_and_gram.1 = (f32[256,1536]{1,0:T(8,128)S(1)}, f32[256,256]{1,0:T(8,128)S(1)}) custom-call(s32[2]{0:T(128)S(1)} %copy-done.2, bf16[2,32,48,128]{3,2,1,0:T(8,128)(2,1)S(1)} %copy-done, f32[32,48,128]{2,1,0:T(8,128)S(1)} %copy-done.1), custom_call_target="tpu_custom_call" | custom-call | tf_op jit(solution)/shard_map/filter_and_gram/pallas_call | solution.py:302
  77.9 0.1 copy.4
  78.0 11.7 %cholesky.50 = f32[128,128]{1,0:T(8,128)S(1)} custom-call(f32[128,128]{1,0:T(8,128)S(1)} %cholesky.118), custom_call_target="Cholesky" | custom-call | tf_op jit(solution)/shard_map/jit(cholesky)/cholesky | solution.py:341
  89.8 9.8 %custom-call.14 = f32[1,128,128]{1,2,0:T(8,128)S(1)} custom-call(f32[1,128,128]{2,1,0:T(8,128)S(1)} %get-tuple-element.30), custom_call_target="InvertDiagBlocksLowerTriangular" | custom-call | tf_op jit(solution)/shard_map/jit(cholesky)/cholesky | solution.py:341
  99.6 0.2 constant_dynamic-update-slice_fusion.1
  99.9 0.3 convolution_subtract_fusion.1
  100.1 11.7 %cholesky.105 = f32[128,128]{1,0:T(8,128)S(1)} custom-call(f32[128,128]{1,0:T(8,128)S(1)} %convolution_subtract_fusion.1), custom_call_target="Cholesky" | custom-call | tf_op jit(solution)/shard_map/jit(cholesky)/cholesky | solution.py:341
  111.9 0.7 compare_reduce_fusion
  113.9 4.1 %while.1 = (s32[]{:T(128)}, f32[256,256]{1,0:T(8,128)S(1)}, s32[2,2]{1,0:T(2,128)S(1)}, f32[2,128,128]{2,1,0:T(8,128)S(1)}, s32[]{:T(128)}) while((s32[]{:T(128)}, f32[256,256]{1,0:T(8,128)S(1)}, s32[2,2]{1,0:T(2,128)S(1)}, f32[2,128,128]{2,1,0:T(8,128)S(1)}, s32[]{:T(128)}) %tuple.23), condition=%wide.while_cond, body=%wide.while_body.sunk | while | flops 2 | bytes 131189 | solution.py:342
  113.9 0.7 fusion.14
  114.6 1.3 bitcast_dynamic-update-slice_fusion.2
  115.9 0.7 fusion.14
  116.6 1.3 bitcast_dynamic-update-slice_fusion.2
  118.0 19.9 %custom-call.15 = f32[2,128,128]{1,2,0:T(8,128)S(1)} custom-call(f32[2,128,128]{2,1,0:T(8,128)S(1)} %get-tuple-element.16), custom_call_target="InvertDiagBlocksLowerTriangular" | custom-call | tf_op jit(solution)/shard_map/triangular_solve | solution.py:342
  137.9 0.8 fusion
  138.7 0.8 convolution_subtract_fusion
  139.5 0.8 fusion.4
  140.4 1.3 maximum_multiply_fusion
  (10 shorter events, 0.2 us)
Async XLA Ops:
  0.1 1.1 copy-start
  1.2 1.1 copy-start.1
  2.3 0.7 copy-start.2

commit v3 on v2

--- a/solution.py
+++ b/solution.py
@@ -70,6 +70,21 @@
     return lax.rem(z + dz, 8) * 16 + lax.rem(y + dy, 4) * 4 + lax.rem(x + dx, 4)
 
 
+def along(me, stride, extent, number):
+    place = lax.rem(lax.div(me, stride), extent)
+    return me + (lax.rem(place + number, extent) - place) * stride
+
+
+def greet(semaphore, me, stride, extent):
+    for number in range(1, extent):
+        pl.semaphore_signal(
+            semaphore,
+            inc=1,
+            device_id={"state": along(me, stride, extent, number)},
+            device_id_type=pl.DeviceIdType.MESH,
+        )
+
+
 def remote(source, target, send, receive, peer):
     return pltpu.make_async_remote_copy(
         src_ref=source,
@@ -91,6 +106,8 @@
     potential_ref,
     rows_ref,
     gram_ref,
+    initial,
+    potential,
     buffers,
     diagonal,
     plane,
@@ -107,6 +124,9 @@
     rows_sem,
     sum_send,
     sum_recv,
+    load_sem,
+    heard_x,
+    heard_y,
 ):
     states, planes, width, _ = states_ref.shape
     rows = width // 8
@@ -114,18 +134,19 @@
     piece = planes * width // devices
     me = lax.axis_index("state")
 
+    loads = [
+        pltpu.make_async_copy(potential_ref, potential, load_sem.at[states]),
+    ] + [
+        pltpu.make_async_copy(states_ref.at[state], initial.at[state], load_sem.at[state])
+        for state in range(states)
+    ]
+    for load in loads:
+        load.start()
+
     barrier = pltpu.get_barrier_semaphore()
-
-    def greet(number, _):
-        pl.semaphore_signal(
-            barrier,
-            inc=1,
-            device_id={"state": neighbour(me, number)},
-            device_id_type=pl.DeviceIdType.MESH,
-        )
-        return 0
-
-    lax.fori_loop(1, devices, greet, 0)
+    greet(barrier, me, 16, 8)
+    greet(barrier, me, 4, 4)
+    greet(barrier, me, 1, 4)
 
     half_width, centre, last_scale = chebyshev_scalars(bounds_ref)
     shift = 3.75 - centre
@@ -134,19 +155,24 @@
 
     def load_potential(z, _):
         for r in range(rows):
-            diagonal[z, r] = 24.0 * (potential_ref[z, pl.ds(r, 8, stride=rows), :] + shift)
-        return 0
-
-    lax.fori_loop(0, planes, load_potential, 0)
+            diagonal[z, r] = 24.0 * (potential[z, pl.ds(r, 8, stride=rows), :] + shift)
+        return 0
+
     for buffer in range(2):
         for z in (0, 1, planes + 2, planes + 3):
             buffers[buffer, z] = zero
+    loads[0].wait()
+    lax.fori_loop(0, planes, load_potential, 0)
+    pl.semaphore_wait(barrier, 7 + 3 + 3)
+    greet(heard_x, me, 1, 4)
+    for load in loads[1:]:
+        load.wait()
     even, odd = buffers.at[0], buffers.at[1]
     matrix = circulant()
 
     def one_state(state, _):
         def load(z, _):
-            plane[...] = states_ref[state, z].astype(jnp.float32)
+            plane[...] = initial[state, z].astype(jnp.float32)
             for r in range(rows):
                 even[z + 2, r] = plane[pl.ds(r, 8, stride=rows), :]
             odd[z + 2] = zero
@@ -157,6 +183,12 @@
         def two_steps(pair, _):
             first = jnp.where(pair == 0, 0.5 * factor, factor)
             filter_step(even, odd, diagonal, matrix, first, None)
+
+            @pl.when((state == 0) & (pair == 3))
+            def _():
+                pl.semaphore_wait(heard_x, 3)
+                greet(heard_y, me, 4, 4)
+
             last = jnp.where(pair == DEGREE // 2 - 1, last_scale, 1.0)
             filter_step(odd, even, diagonal, matrix, factor, last)
             return 0
@@ -172,7 +204,7 @@
 
         @pl.when(state == 0)
         def _():
-            pl.semaphore_wait(barrier, devices - 1)
+            pl.semaphore_wait(heard_y, 3)
 
         def send(number, _):
             peer = neighbour(me, number)
@@ -307,11 +339,13 @@
         ],
         in_specs=[
             pl.BlockSpec(memory_space=pltpu.SMEM),
-            pl.BlockSpec(memory_space=pltpu.VMEM),
-            pl.BlockSpec(memory_space=pltpu.VMEM),
+            pl.BlockSpec(memory_space=pl.ANY),
+            pl.BlockSpec(memory_space=pl.ANY),
         ],
         out_specs=[pl.BlockSpec(memory_space=pl.ANY), pl.BlockSpec(memory_space=pltpu.VMEM)],
         scratch_shapes=[
+            pltpu.VMEM(states.shape, states.dtype),
+            pltpu.VMEM(potential.shape, potential.dtype),
             pltpu.VMEM((2, planes + 4, width // 8, 8, GY), jnp.float32),
             pltpu.VMEM((planes, width // 8, 8, GY), jnp.float32),
             pltpu.VMEM((width, GY), jnp.float32),
@@ -328,19 +362,134 @@
             pltpu.SemaphoreType.DMA,
             pltpu.SemaphoreType.DMA((3,)),
             pltpu.SemaphoreType.DMA((3,)),
+            pltpu.SemaphoreType.DMA((count + 1,)),
+            pltpu.SemaphoreType.REGULAR,
+            pltpu.SemaphoreType.REGULAR,
         ],
         compiler_params=pltpu.CompilerParams(
-            vmem_limit_bytes=40 << 20, collective_id=0, has_side_effects=True
+            vmem_limit_bytes=56 << 20, collective_id=0, has_side_effects=True
         ),
         name="filter_and_gram",
     )(bounds, states, potential)
 
 
+def times(left, right, left_dim, right_dim):
+    return lax.dot_general(
+        left,
+        right,
+        (((left_dim,), (right_dim,)), ((), ())),
+        precision=lax.Precision.HIGHEST,
+        preferred_element_type=jnp.float32,
+    )
+
+
+def inverse_factor(tiles):
+    row = lax.broadcasted_iota(jnp.int32, (8, 128), 0)
+    lane = lax.broadcasted_iota(jnp.int32, (8, 128), 1)
+
+    def of_row(value, index):
+        return jnp.broadcast_to(value[index : index + 1, :], (8, 128))
+
+    def of_lane(value, index):
+        return jnp.broadcast_to(value[:, index : index + 1], (8, 128))
+
+    tiles = list(tiles)
+    result = []
+    for tile in range(16):
+        start = 8 * tile
+        here = tiles[tile]
+        solved = jnp.zeros((8, 128), jnp.float32)
+        columns = [of_lane(here, start + c) for c in range(8)]
+        below = range(tile + 1, 16)
+        multipliers = [[of_lane(tiles[i], start + c) for c in range(8)] for i in below]
+        for i in range(8):
+            pivot = of_row(columns[i], i)
+            root = lax.rsqrt(pivot)
+            root = root * (1.5 - 0.5 * pivot * root * root)
+            inverse = root * root
+            here = jnp.where(lane == start + i, jnp.where(row == i, 1.0, 0.0), here)
+            pivot_row = of_row(here, i)
+            solved = jnp.where(row == i, pivot_row * root, solved)
+            others = jnp.where(row == i, 0.0, columns[i])
+            scaled = pivot_row * inverse
+            here = jnp.where(row == i, scaled, here - others * scaled)
+            for c in range(i + 1, 8):
+                entry = of_row(columns[c], i) * inverse
+                columns[c] = jnp.where(row == i, entry, columns[c] - others * entry)
+        result.append(jnp.where(lane <= start + row, solved, 0.0))
+        spread = [of_row(here, c) for c in range(8)]
+        for multiplier, i in zip(multipliers, below):
+            parts = [multiplier[c] * spread[c] for c in range(8)]
+            total = ((parts[0] + parts[1]) + (parts[2] + parts[3])) + (
+                (parts[4] + parts[5]) + (parts[6] + parts[7])
+            )
+            tiles[i] = jnp.where((lane >= start) & (lane < start + 8), 0.0, tiles[i]) - total
+    return result
+
+
+def factor_and_solve_kernel(
+    gram_ref, rows_ref, out_ref, work, inverses, low, rows, out, rows_sem, out_sem, *, scale
+):
+    half = gram_ref.shape[0] // 2
+    width = rows_ref.shape[1]
+    load = pltpu.make_async_copy(rows_ref, rows, rows_sem)
+    load.start()
+    work[...] = gram_ref[0:half, 0:half]
+
+    def one_half(number, _):
+        tiles = inverse_factor([work[8 * i : 8 * i + 8] for i in range(16)])
+        for i in range(16):
+            inverses[number, 8 * i : 8 * i + 8] = tiles[i]
+
+        @pl.when(number == 0)
+        def _():
+            low[...] = times(gram_ref[half:, 0:half], inverses[0], 1, 1)
+            work[...] = gram_ref[half:, half:] - times(low[...], low[...], 1, 1)
+
+        return 0
+
+    lax.fori_loop(0, 2, one_half, 0)
+    first, second = inverses[0] * scale, inverses[1] * scale
+    between = -times(times(second, low[...], 1, 0), inverses[0], 1, 0)
+    load.wait()
+    pieces = out_sem.shape[0]
+    stores = []
+    for piece in range(pieces):
+        here = pl.ds(piece * width // pieces, width // pieces)
+        upper, lower = rows[0:half, here], rows[half:, here]
+        out[0:half, here] = times(first, upper, 1, 0)
+        out[half:, here] = times(between, upper, 1, 0) + times(second, lower, 1, 0)
+        store = pltpu.make_async_copy(out.at[:, here], out_ref.at[:, here], out_sem.at[piece])
+        store.start()
+        stores.append(store)
+    for store in stores:
+        store.wait()
+
+
+def factor_and_solve(gram, rows, scale):
+    half = gram.shape[0] // 2
+    return pl.pallas_call(
+        functools.partial(factor_and_solve_kernel, scale=scale),
+        out_shape=jax.ShapeDtypeStruct(rows.shape, jnp.float32),
+        in_specs=[pl.BlockSpec(memory_space=pltpu.VMEM), pl.BlockSpec(memory_space=pl.ANY)],
+        out_specs=pl.BlockSpec(memory_space=pl.ANY),
+        scratch_shapes=[
+            pltpu.VMEM((half, half), jnp.float32),
+            pltpu.VMEM((2, half, half), jnp.float32),
+            pltpu.VMEM((half, half), jnp.float32),
+            pltpu.VMEM(rows.shape, jnp.float32),
+            pltpu.VMEM(rows.shape, jnp.float32),
+            pltpu.SemaphoreType.DMA,
+            pltpu.SemaphoreType.DMA((4,)),
+        ],
+        compiler_params=pltpu.CompilerParams(vmem_limit_bytes=56 << 20),
+        name="factor_and_solve",
+    )(gram, rows)
+
+
 def per_device(initial_states, potential, bounds):
     row_block, gram = filter_and_gram(initial_states, potential, bounds)
-    factor = jnp.linalg.cholesky(gram)
-    solved = lax.linalg.triangular_solve(factor, row_block, left_side=True, lower=True)
-    return solved * math.sqrt(math.prod(initial_states.shape[1:]))
+    return factor_and_solve(gram, row_block, math.sqrt(math.prod(initial_states.shape[1:])))
 
 
 def solution(mesh):

time: 142 us -> 92.8 us (0.65)
  other arithmetic: 55.3 us -> 0 us
  Pallas kernels: 74.8 us -> 92.6 us
  local copies, waits for them, and re-layouts: 7.17 us -> 0 us
  matrix products: 2.93 us -> 0 us
    another operation x9 -> x0, other arithmetic: 54 us -> none  [the longest x6 34 us: per_device(): factor = jnp.linalg.cholesky(gram)]
    pallas_call x0 -> x1, Pallas kernels: none -> 16.3 us  [factor_and_solve(): pl.pallas_call(functools.partial(factor_and_solve_kernel, scale=scale), o...]
    another operation x9 -> x0, local copies, waits for them, and re-layouts: 4.12 us -> none
    another operation x5 -> x0, matrix products: 2.93 us -> none  [the longest x3 2.46 us: per_device(): lax.linalg.triangular_solve(factor, row_block, left_side=True, lower=True)]
    unnamed x6 -> x0, local copies, waits for them, and re-layouts: 2.92 us -> none
    pallas_call x1, Pallas kernels: 74.8 us -> 76.4 us  [filter_and_gram(): pl.pallas_call(filter_gram_kernel, out_shape=[jax.ShapeDtypeStruct((total...]
where the time goes in v3:
time: 92.8 us; the launch traced here: 92.7 us
  Pallas kernels  92.6 us (100%)
    pallas_call x1, Pallas kernels, filter_and_gram(): pl.pallas_call(filter_gram_kernel, out_shape=[jax.ShapeDtypeStruct((total...  76.4 us
    pallas_call x1, Pallas kernels, factor_and_solve(): pl.pallas_call(functools.partial(factor_and_solve_kernel, scale=scale), o...  16.3 us

profile of v3, /device:TPU:8, one launch (start us, length us, event | category | flops | bytes accessed | tf_op | source)
XLA Modules:
  0.0 92.7 jit_solution(1698626519183936690)
XLA Ops:
  0.0 76.4 %filter_and_gram.1 = (f32[256,1536]{1,0:T(8,128)}, f32[256,256]{1,0:T(8,128)}) custom-call(s32[2]{0:T(128)} %bounds_ref.1, bf16[2,32,48,128]{3,2,1,0:T(8,128)(2,1)} %states_ref.1, f32[32,48,128]{2,1,0:T(8,128)} %potential_ref.1), custom_call_target="tpu_custom_call" | custom-call | tf_op jit(solution)/shard_map/filter_and_gram/pallas_call | solution.py:334
  76.4 16.3 %factor_and_solve.1 = f32[256,1536]{1,0:T(8,128)} custom-call(f32[256,256]{1,0:T(8,128)} %get-tuple-element.7.gram_ref, f32[256,1536]{1,0:T(8,128)} %get-tuple-element.8.rows_ref), custom_call_target="tpu_custom_call" | custom-call | tf_op jit(solution)/shard_map/factor_and_solve/pallas_call | solution.py:471

commit v4 on v3

v4 whole, which is shorter than its diff:
```python
import functools
import math

import jax
import jax.numpy as jnp
from jax import lax
from jax.experimental import pallas as pl
from jax.experimental.pallas import tpu as pltpu
from jax.sharding import PartitionSpec as P

DEGREE = 16
ANCHOR_VALUE = -1.125
XB = 8
GY = 128


def chebyshev_scalars(bounds_ref):
    low_end = jnp.full((8, GY), bounds_ref[0].astype(jnp.float32), jnp.float32) / 64.0
    high_end = jnp.full((8, GY), bounds_ref[1].astype(jnp.float32), jnp.float32) / 16.0
    half_width = (high_end - low_end) / 2.0
    centre = (high_end + low_end) / 2.0
    place = (ANCHOR_VALUE - centre) / half_width
    before, now = jnp.ones_like(place), place
    for _ in range(DEGREE - 1):
        before, now = now, 2.0 * place * now - before
    return half_width, centre, 1.0 / now


def circulant():
    row = lax.rem(lax.broadcasted_iota(jnp.int32, (2 * GY, GY), 0), GY)
    column = lax.broadcasted_iota(jnp.int32, (2 * GY, GY), 1)
    apart = lax.rem(row - column + GY, GY)
    near = jnp.where((apart == 1) | (apart == GY - 1), -16.0, 0.0)
    far = jnp.where((apart == 2) | (apart == GY - 2), 1.0, 0.0)
    return (near + far).astype(jnp.bfloat16)


def filter_step(source, target, diagonal, matrix, factor, scale):
    planes, rows = diagonal.shape[0], diagonal.shape[1]
    values = source[pl.ds(2, planes)].reshape(planes * rows * 8, GY)
    high = values.astype(jnp.bfloat16)
    low = (values - high.astype(jnp.float32)).astype(jnp.bfloat16)
    along_y = jnp.dot(
        jnp.concatenate([high, low], 1), matrix, preferred_element_type=jnp.float32
    ).reshape(planes, rows, 8, GY)
    for z in range(planes):
        here = [source[z + 2, r] for r in range(rows)]
        ring = (
            [pltpu.roll(here[r], 1, 0) for r in (rows - 2, rows - 1)]
            + here
            + [pltpu.roll(here[r], 7, 0) for r in (0, 1)]
        )
        for r in range(rows):
            near = (source[z + 1, r] + source[z + 3, r]) + (ring[r + 1] + ring[r + 3])
            far = (source[z, r] + source[z + 4, r]) + (ring[r] + ring[r + 4])
            total = far - 16.0 * near + diagonal[z, r] * here[r] + along_y[z, r]
            latest = factor * total - target[z + 2, r]
            if scale is not None:
                latest = latest * scale
            target[z + 2, r] = latest


GROUP = 4
PLANES_Z = 8
PLANE_XY = 16


def neighbour(me, number):
    dz, dy, dx = lax.rem(number, 8), lax.rem(lax.div(number, 8), 4), lax.div(number, 32)
    z, y, x = lax.div(me, 16), lax.rem(lax.div(me, 4), 4), lax.rem(me, 4)
    return lax.rem(z + dz, 8) * 16 + lax.rem(y + dy, 4) * 4 + lax.rem(x + dx, 4)


def along(me, stride, extent, number):
    place = lax.rem(lax.div(me, stride), extent)
    return me + (lax.rem(place + number, extent) - place) * stride


def greet(semaphore, me, stride, extent):
    for number in range(1, extent):
        pl.semaphore_signal(
            semaphore,
            inc=1,
            device_id={"state": along(me, stride, extent, number)},
            device_id_type=pl.DeviceIdType.MESH,
        )


def remote(source, target, send, receive, peer):
    return pltpu.make_async_remote_copy(
        src_ref=source,
        dst_ref=target,
        send_sem=send,
        recv_sem=receive,
        device_id={"state": peer},
        device_id_type=pl.DeviceIdType.MESH,
    )


def wait_bytes(ref, semaphore):
    pltpu.make_async_copy(ref, ref, semaphore).wait()


def filter_gram_kernel(
    bounds_ref,
    states_ref,
    potential_ref,
    rows_ref,
    first_ref,
    low_ref,
    rest_ref,
    initial,
    potential,
    buffers,
    diagonal,
    plane,
    outbox,
    inbox,
    block,
    partial_first,
    partial_rest,
    plane_first,
    plane_rest,
    column_first,
    column_rest,
    gathered_first,
    gathered_rest,
    send_sem,
    recv_sem,
    own_sem,
    rows_sem,
    sum_send,
    sum_recv,
    load_sem,
    heard_x,
    heard_y,
):
    partial, in_plane = (partial_first, partial_rest), (plane_first, plane_rest)
    in_column, gathered = (column_first, column_rest), (gathered_first, gathered_rest)
    states, planes, width, _ = states_ref.shape
    rows = width // 8
    devices = 128
    piece = planes * width // devices
    me = lax.axis_index("state")

    loads = [
        pltpu.make_async_copy(potential_ref, potential, load_sem.at[states]),
    ] + [
        pltpu.make_async_copy(states_ref.at[state], initial.at[state], load_sem.at[state])
        for state in range(states)
    ]
    for load in loads:
        load.start()

    barrier = pltpu.get_barrier_semaphore()
    greet(barrier, me, 16, 8)
    greet(barrier, me, 4, 4)
    greet(barrier, me, 1, 4)

    half_width, centre, last_scale = chebyshev_scalars(bounds_ref)
    shift = 3.75 - centre
    factor = 2.0 / (24.0 * half_width)
    zero = jnp.zeros((rows, 8, GY), jnp.float32)

    def load_potential(group, _):
        for part in range(GROUP):
            z = group * GROUP + part
            for r in range(rows):
                diagonal[z, r] = 24.0 * (potential[z, pl.ds(r, 8, stride=rows), :] + shift)
        return 0

    for buffer in range(2):
        for z in (0, 1, planes + 2, planes + 3):
            buffers[buffer, z] = zero
    loads[0].wait()
    lax.fori_loop(0, planes // GROUP, load_potential, 0)
    pl.semaphore_wait(barrier, 7 + 3 + 3)
    greet(heard_x, me, 1, 4)
    loads[1].wait()
    even, odd = buffers.at[0], buffers.at[1]
    matrix = circulant()

    def one_state(state, _):
        def load(group, _):
            for part in range(GROUP):
                plane[part] = initial[state, group * GROUP + part].astype(jnp.float32)
            for part in range(GROUP):
                z = group * GROUP + part
                for r in range(rows):
                    even[z + 2, r] = plane[part, pl.ds(r, 8, stride=rows), :]
                odd[z + 2] = zero
            return 0

        lax.fori_loop(0, planes // GROUP, load, 0)

        def two_steps(pair, _):
            first = jnp.where(pair == 0, 0.5 * factor, factor)
            filter_step(even, odd, diagonal, matrix, first, None)

            @pl.when((state == 0) & (pair == 3))
            def _():
                pl.semaphore_wait(heard_x, 3)
                greet(heard_y, me, 4, 4)
                for load in loads[2:]:
                    load.wait()

            last = jnp.where(pair == DEGREE // 2 - 1, last_scale, 1.0)
            filter_step(odd, even, diagonal, matrix, factor, last)
            return 0

        lax.fori_loop(0, DEGREE // 2, two_steps, 0)

        def store(group, _):
            for part in range(GROUP):
                z = group * GROUP + part
                for r in range(rows):
                    outbox[pl.ds((state * planes + z) * width + r, 8, stride=rows), :] = even[z + 2, r]
            return 0

        lax.fori_loop(0, planes // GROUP, store, 0)

        @pl.when(state == 0)
        def _():
            pl.semaphore_wait(heard_y, 3)

        def send(number, _):
            peer = neighbour(me, number)
            remote(
                outbox.at[pl.ds((state * devices + peer) * piece, piece)],
                inbox.at[pl.ds((me * states + state) * piece, piece)],
                send_sem,
                recv_sem,
                peer,
            ).start()
            return 0

        lax.fori_loop(1, devices, send, 0)
        pltpu.make_async_copy(
            outbox.at[pl.ds((state * devices + me) * piece, piece)],
            inbox.at[pl.ds((me * states + state) * piece, piece)],
            own_sem.at[state],
        ).start()
        return 0

    lax.fori_loop(0, states, one_state, 0)
    for state in range(states):
        pltpu.make_async_copy(
            outbox.at[pl.ds((state * devices + me) * piece, piece)],
            inbox.at[pl.ds((me * states + state) * piece, piece)],
            own_sem.at[state],
        ).wait()
    wait_bytes(inbox.at[pl.ds(0, (devices - 1) * states * piece)], recv_sem)
    wait_bytes(outbox.at[pl.ds(0, (devices - 1) * states * piece)], send_sem)

    total = devices * states

    def gram_piece(column, _):
        here = inbox[pl.ds(column, total, stride=piece), :]
        block[:, pl.ds(pl.multiple_of(column * GY, GY), GY)] = here
        return 0

    lax.fori_loop(0, piece, gram_piece, 0)
    rows_copy = pltpu.make_async_copy(block, rows_ref, rows_sem)
    rows_copy.start()
    half = total // 2

    mine, level = lax.rem(me, PLANE_XY), lax.div(me, PLANE_XY)

    def part_of(ref, number):
        count = ref.shape[0] // PLANE_XY
        return pl.ds(pl.multiple_of(number * count, 8), count)

    def plane_peer(number):
        y, x = lax.div(mine, 4), lax.rem(mine, 4)
        return lax.rem(y + lax.div(number, 4), 4) * 4 + lax.rem(x + lax.rem(number, 4), 4)

    def first_round(which):
        source, target = partial[which], in_plane[which]

        def share(number, _):
            to = plane_peer(number)
            remote(
                source.at[part_of(source, to)],
                target.at[mine],
                sum_send.at[which, 0],
                sum_recv.at[which, 0],
                level * PLANE_XY + to,
            ).start()
            return 0

        lax.fori_loop(1, PLANE_XY, share, 0)
        target[mine] = source[part_of(source, mine), :]

    def total_of(ref):
        parts = [ref[number] for number in range(ref.shape[0])]
        while len(parts) > 1:
            parts = [parts[i] + parts[i + 1] for i in range(0, len(parts), 2)]
        return parts[0]

    def second_round(which):
        source, target = in_plane[which], in_column[which]
        wait_bytes(source.at[pl.ds(0, PLANE_XY - 1)], sum_recv.at[which, 0])
        target[level] = total_of(source)

        def along_z(number, _):
            remote(
                target.at[level],
                target.at[level],
                sum_send.at[which, 1],
                sum_recv.at[which, 1],
                lax.rem(level + number, PLANES_Z) * PLANE_XY + mine,
            ).start()
            return 0

        lax.fori_loop(1, PLANES_Z, along_z, 0)

    def third_round(which):
        source, target = in_column[which], gathered[which]
        wait_bytes(source.at[pl.ds(0, PLANES_Z - 1)], sum_recv.at[which, 1])
        here = part_of(target, mine)
        target[here, :] = total_of(source)

        def spread(number, _):
            remote(
                target.at[here],
                target.at[here],
                sum_send.at[which, 2],
                sum_recv.at[which, 2],
                level * PLANE_XY + plane_peer(number),
            ).start()
            return 0

        lax.fori_loop(1, PLANE_XY, spread, 0)

    def most_of(ref):
        return ref.at[pl.ds(0, ref.shape[0] // PLANE_XY * (PLANE_XY - 1))]

    partial[0][...] = times(block[0:half], block[0:half], 1, 1)
    first_round(0)
    partial[1][0:half] = times(block[half:], block[0:half], 1, 1)
    partial[1][half:] = times(block[half:], block[half:], 1, 1)
    first_round(1)
    second_round(0)
    second_round(1)
    third_round(0)
    third_round(1)
    wait_bytes(most_of(gathered[0]), sum_recv.at[0, 2])
    tiles = inverse_factor([gathered[0][8 * i : 8 * i + 8] for i in range(16)])
    for i in range(16):
        first_ref[8 * i : 8 * i + 8] = tiles[i]
    wait_bytes(most_of(gathered[1]), sum_recv.at[1, 2])
    low = times(gathered[1][0:half], first_ref[...], 1, 1)
    low_ref[...] = low
    rest_ref[...] = gathered[1][half:] - times(low, low, 1, 1)
    for which in range(2):
        wait_bytes(in_plane[which].at[pl.ds(0, PLANE_XY - 1)], sum_send.at[which, 0])
        wait_bytes(in_column[which].at[pl.ds(0, PLANES_Z - 1)], sum_send.at[which, 1])
        wait_bytes(most_of(gathered[which]), sum_send.at[which, 2])
    rows_copy.wait()


def filter_and_gram(states, potential, bounds):
    count, planes, width = states.shape[:3]
    total, half = count * 128, count * 64
    points = planes * width * GY // 128
    return pl.pallas_call(
        filter_gram_kernel,
        out_shape=[
            jax.ShapeDtypeStruct((total, points), jnp.float32),
            jax.ShapeDtypeStruct((half, half), jnp.float32),
            jax.ShapeDtypeStruct((half, half), jnp.float32),
            jax.ShapeDtypeStruct((half, half), jnp.float32),
        ],
        in_specs=[
            pl.BlockSpec(memory_space=pltpu.SMEM),
            pl.BlockSpec(memory_space=pl.ANY),
            pl.BlockSpec(memory_space=pl.ANY),
        ],
        out_specs=[pl.BlockSpec(memory_space=pl.ANY)] + [pl.BlockSpec(memory_space=pltpu.VMEM)] * 3,
        scratch_shapes=[
            pltpu.VMEM(states.shape, states.dtype),
            pltpu.VMEM(potential.shape, potential.dtype),
            pltpu.VMEM((2, planes + 4, width // 8, 8, GY), jnp.float32),
            pltpu.VMEM((planes, width // 8, 8, GY), jnp.float32),
            pltpu.VMEM((GROUP, width, GY), jnp.float32),
            pltpu.VMEM((count * planes * width, GY), jnp.float32),
            pltpu.VMEM((count * planes * width, GY), jnp.float32),
            pltpu.VMEM((total, points), jnp.float32),
            pltpu.VMEM((half, GY), jnp.float32),
            pltpu.VMEM((total, GY), jnp.float32),
            pltpu.VMEM((PLANE_XY, half // PLANE_XY, GY), jnp.float32),
            pltpu.VMEM((PLANE_XY, total // PLANE_XY, GY), jnp.float32),
            pltpu.VMEM((PLANES_Z, half // PLANE_XY, GY), jnp.float32),
            pltpu.VMEM((PLANES_Z, total // PLANE_XY, GY), jnp.float32),
            pltpu.VMEM((half, GY), jnp.float32),
            pltpu.VMEM((total, GY), jnp.float32),
            pltpu.SemaphoreType.DMA,
            pltpu.SemaphoreType.DMA,
            pltpu.SemaphoreType.DMA((count,)),
            pltpu.SemaphoreType.DMA,
            pltpu.SemaphoreType.DMA((2, 3)),
            pltpu.SemaphoreType.DMA((2, 3)),
            pltpu.SemaphoreType.DMA((count + 1,)),
            pltpu.SemaphoreType.REGULAR,
            pltpu.SemaphoreType.REGULAR,
        ],
        compiler_params=pltpu.CompilerParams(
            vmem_limit_bytes=56 << 20, collective_id=0, has_side_effects=True
        ),
        name="filter_and_gram",
    )(bounds, states, potential)


def times(left, right, left_dim, right_dim):
    return lax.dot_general(
        left,
        right,
        (((left_dim,), (right_dim,)), ((), ())),
        precision=lax.Precision.HIGHEST,
        preferred_element_type=jnp.float32,
    )


def inverse_factor(tiles, beside=None):
    row = lax.broadcasted_iota(jnp.int32, (8, 128), 0)
    lane = lax.broadcasted_iota(jnp.int32, (8, 128), 1)

    def of_row(value, index):
        return jnp.broadcast_to(value[index : index + 1, :], (8, 128))

    def of_lane(value, index):
        return jnp.broadcast_to(value[:, index : index + 1], (8, 128))

    tiles = list(tiles)
    result = []
    for tile in range(16):
        start = 8 * tile
        here = tiles[tile]
        solved = jnp.zeros((8, 128), jnp.float32)
        columns = [of_lane(here, start + c) for c in range(8)]
        below = range(tile + 1, 16)
        multipliers = [[of_lane(tiles[i], start + c) for c in range(8)] for i in below]
        inverses = []
        for i in range(8):
            pivot = of_row(columns[i], i)
            inverses.append(1.0 / pivot)
            here = jnp.where(lane == start + i, jnp.where(row == i, 1.0, 0.0), here)
            pivot_row = of_row(here, i)
            solved = jnp.where(row == i, pivot_row * lax.rsqrt(pivot), solved)
            others = jnp.where(row == i, 0.0, columns[i]) * inverses[i]
            here = here - others * pivot_row
            for c in range(i + 1, 8):
                columns[c] = columns[c] - others * of_row(columns[c], i)
        result.append(jnp.where(lane <= start + row, solved, 0.0))
        spread = [of_row(here, c) * inverses[c] for c in range(8)]
        for multiplier, i in zip(multipliers, below):
            parts = [multiplier[c] * spread[c] for c in range(8)]
            total = ((parts[0] + parts[1]) + (parts[2] + parts[3])) + (
                (parts[4] + parts[5]) + (parts[6] + parts[7])
            )
            tiles[i] = jnp.where((lane >= start) & (lane < start + 8), 0.0, tiles[i]) - total
        if beside is not None:
            beside(tile)
    return result


def solve_kernel(
    first_ref, low_ref, rest_ref, rows_ref, out_ref, second, rows, out, rows_sem, out_sem, *, scale
):
    half = first_ref.shape[0]
    width = rows_ref.shape[1]
    load = pltpu.make_async_copy(rows_ref, rows, rows_sem)
    load.start()
    first_piece = 16 - width // 128

    def beside(tile):
        if tile < first_piece:
            return
        if tile == first_piece:
            load.wait()
        here = pl.ds((tile - first_piece) * 128, 128)
        upper = times(first_ref[...], rows[0:half, here], 1, 0)
        out[0:half, here] = upper * scale
        rows[half:, here] = rows[half:, here] - times(low_ref[...], upper, 1, 0)

    tiles = inverse_factor([rest_ref[8 * i : 8 * i + 8] for i in range(16)], beside)
    upper_store = pltpu.make_async_copy(
        out.at[0:half], out_ref.at[0:half], out_sem.at[out_sem.shape[0] - 1]
    )
    upper_store.start()
    for i in range(16):
        second[8 * i : 8 * i + 8] = tiles[i] * scale
    pieces = out_sem.shape[0] - 1
    stores = [upper_store]
    for piece in range(pieces):
        here = pl.ds(piece * width // pieces, width // pieces)
        out[half:, here] = times(second[...], rows[half:, here], 1, 0)
        store = pltpu.make_async_copy(
            out.at[half:, here], out_ref.at[half:, here], out_sem.at[piece]
        )
        store.start()
        stores.append(store)
    for store in stores:
        store.wait()


def solve(first, low, rest, rows, scale):
    half = first.shape[0]
    return pl.pallas_call(
        functools.partial(solve_kernel, scale=scale),
        out_shape=jax.ShapeDtypeStruct(rows.shape, jnp.float32),
        in_specs=[pl.BlockSpec(memory_space=pltpu.VMEM)] * 3 + [pl.BlockSpec(memory_space=pl.ANY)],
        out_specs=pl.BlockSpec(memory_space=pl.ANY),
        scratch_shapes=[
            pltpu.VMEM((half, half), jnp.float32),
            pltpu.VMEM(rows.shape, jnp.float32),
            pltpu.VMEM(rows.shape, jnp.float32),
            pltpu.SemaphoreType.DMA,
            pltpu.SemaphoreType.DMA((4,)),
        ],
        compiler_params=pltpu.CompilerParams(vmem_limit_bytes=56 << 20),
        name="solve",
    )(first, low, rest, rows)


def per_device(initial_states, potential, bounds):
    row_block, first, low, rest = filter_and_gram(initial_states, potential, bounds)
    return solve(first, low, rest, row_block, math.sqrt(math.prod(initial_states.shape[1:])))


def solution(mesh):
    return jax.shard_map(
        per_device,
        mesh=mesh,
        in_specs=(P(("cuts", "state"), None, None, None), P(), P("cuts")),
        out_specs=P("cuts", "state"),
        check_vma=False,
    )
```

time: 92.8 us -> 87.3 us (0.941)
  Pallas kernels: 92.6 us -> 86.9 us
    pallas_call x1, Pallas kernels: 16.3 us -> 8.31 us  [solve(): pl.pallas_call(functools.partial(solve_kernel, scale=scale), out_shape=ja...]
    pallas_call x1, Pallas kernels: 76.4 us -> 78.6 us  [filter_and_gram(): pl.pallas_call(filter_gram_kernel, out_shape=[jax.ShapeDtypeStruct((total...]
where the time goes in v4:
time: 87.3 us; the launch traced here: 86.9 us
  Pallas kernels  86.9 us (100%)
    pallas_call x1, Pallas kernels, filter_and_gram(): pl.pallas_call(filter_gram_kernel, out_shape=[jax.ShapeDtypeStruct((total...  78.6 us
    pallas_call x1, Pallas kernels, solve(): pl.pallas_call(functools.partial(solve_kernel, scale=scale), out_shape=ja...  8.31 us

profile of v4, /device:TPU:8, one launch (start us, length us, event | category | flops | bytes accessed | tf_op | source)
XLA Modules:
  0.0 86.9 jit_solution(10143889230235649654)
XLA Ops:
  0.0 78.6 %filter_and_gram.1 = (f32[256,1536]{1,0:T(8,128)}, f32[128,128]{1,0:T(8,128)}, f32[128,128]{1,0:T(8,128)}, f32[128,128]{1,0:T(8,128)}) custom-call(s32[2]{0:T(128)} %bounds_ref.1, bf16[2,32,48,128]{3,2,1,0:T(8,128)(2,1)} %states_ref.1, f32[32,48,128]{2,1,0:T(8,128)} %potential_ref.1), custom_call_target="tpu_custom_call" | custom-call | tf_op jit(solution)/shard_map/filter_and_gram/pallas_call | solution.py:366
  78.6 8.3 %solve.1 = f32[256,1536]{1,0:T(8,128)} custom-call(f32[128,128]{1,0:T(8,128)} %get-tuple-element.9.first_ref, f32[128,128]{1,0:T(8,128)} %get-tuple-element.10.low_ref, f32[128,128]{1,0:T(8,128)} %get-tuple-element.11.rest_ref, f32[256,1536]{1,0:T(8,128)} %get-tuple-element.12.rows_ref), custom_call_target="tpu_custom_call" | custom-call | tf_op jit(solution)/shard_map/solve/pallas_call | solution.py:509

commit v5 on v4

--- a/solution.py
+++ b/solution.py
@@ -65,12 +65,6 @@
 PLANE_XY = 16
 
 
-def neighbour(me, number):
-    dz, dy, dx = lax.rem(number, 8), lax.rem(lax.div(number, 8), 4), lax.div(number, 32)
-    z, y, x = lax.div(me, 16), lax.rem(lax.div(me, 4), 4), lax.rem(me, 4)
-    return lax.rem(z + dz, 8) * 16 + lax.rem(y + dy, 4) * 4 + lax.rem(x + dx, 4)
-
-
 def along(me, stride, extent, number):
     place = lax.rem(lax.div(me, stride), extent)
     return me + (lax.rem(place + number, extent) - place) * stride
@@ -113,7 +107,7 @@
     potential,
     buffers,
     diagonal,
-    plane,
+    start,
     outbox,
     inbox,
     block,
@@ -132,6 +126,7 @@
     sum_send,
     sum_recv,
     load_sem,
+    lend_sem,
     heard_x,
     heard_y,
 ):
@@ -174,20 +169,37 @@
             buffers[buffer, z] = zero
     loads[0].wait()
     lax.fori_loop(0, planes // GROUP, load_potential, 0)
-    pl.semaphore_wait(barrier, 7 + 3 + 3)
-    greet(heard_x, me, 1, 4)
-    loads[1].wait()
     even, odd = buffers.at[0], buffers.at[1]
     matrix = circulant()
-
-    def one_state(state, _):
+    toward = jnp.where(lax.axis_index("cuts") == 0, 1, -1)
+    mine, level = lax.rem(me, PLANE_XY), lax.div(me, PLANE_XY)
+
+    def at_level(number):
+        return lax.rem(level + number + PLANES_Z, PLANES_Z) * PLANE_XY
+
+    def to_float(state):
+        def convert(group, _):
+            for part in range(GROUP):
+                z = group * GROUP + part
+                start[state, z] = initial[state, z].astype(jnp.float32)
+            return 0
+
+        lax.fori_loop(0, planes // GROUP, convert, 0)
+
+    lend = remote(start.at[1], start.at[2], lend_sem.at[0], lend_sem.at[1], at_level(toward) + mine)
+    loads[1].wait()
+    to_float(0)
+
+    def one_turn(turn, _):
+        @pl.when(turn == 2)
+        def _():
+            lend.wait()
+
         def load(group, _):
-            for part in range(GROUP):
-                plane[part] = initial[state, group * GROUP + part].astype(jnp.float32)
             for part in range(GROUP):
                 z = group * GROUP + part
                 for r in range(rows):
-                    even[z + 2, r] = plane[part, pl.ds(r, 8, stride=rows), :]
+                    even[z + 2, r] = start[turn, z, pl.ds(r, 8, stride=rows), :]
                 odd[z + 2] = zero
             return 0
 
@@ -197,12 +209,18 @@
             first = jnp.where(pair == 0, 0.5 * factor, factor)
             filter_step(even, odd, diagonal, matrix, first, None)
 
-            @pl.when((state == 0) & (pair == 3))
+            @pl.when((turn == 0) & (pair == 1))
+            def _():
+                pl.semaphore_wait(barrier, 7 + 3 + 3)
+                greet(heard_x, me, 1, 4)
+                loads[2].wait()
+                to_float(1)
+                lend.start()
+
+            @pl.when((turn == 0) & (pair == 4))
             def _():
                 pl.semaphore_wait(heard_x, 3)
                 greet(heard_y, me, 4, 4)
-                for load in loads[2:]:
-                    load.wait()
 
             last = jnp.where(pair == DEGREE // 2 - 1, last_scale, 1.0)
             filter_step(odd, even, diagonal, matrix, factor, last)
@@ -214,43 +232,57 @@
             for part in range(GROUP):
                 z = group * GROUP + part
                 for r in range(rows):
-                    outbox[pl.ds((state * planes + z) * width + r, 8, stride=rows), :] = even[z + 2, r]
+                    outbox[pl.ds((turn * planes + z) * width + r, 8, stride=rows), :] = even[z + 2, r]
             return 0
 
         lax.fori_loop(0, planes // GROUP, store, 0)
 
-        @pl.when(state == 0)
+        @pl.when(turn == 0)
         def _():
             pl.semaphore_wait(heard_y, 3)
 
-        def send(number, _):
-            peer = neighbour(me, number)
-            remote(
-                outbox.at[pl.ds((state * devices + peer) * piece, piece)],
-                inbox.at[pl.ds((me * states + state) * piece, piece)],
-                send_sem,
-                recv_sem,
-                peer,
-            ).start()
-            return 0
-
-        lax.fori_loop(1, devices, send, 0)
-        pltpu.make_async_copy(
-            outbox.at[pl.ds((state * devices + me) * piece, piece)],
-            inbox.at[pl.ds((me * states + state) * piece, piece)],
-            own_sem.at[state],
-        ).start()
+        depth = jnp.where(turn == 0, PLANES_Z, PLANES_Z // 2)
+        heading = jnp.where(turn == 1, -toward, toward)
+        y, x = lax.div(mine, 4), lax.rem(mine, 4)
+
+        def send_column(column, _):
+            beside = lax.rem(y + lax.div(column, 4), 4) * 4 + lax.rem(x + lax.rem(column, 4), 4)
+
+            def send(number, _):
+                peer = at_level(number * heading) + beside
+                remote(
+                    outbox.at[pl.ds((turn * devices + peer) * piece, piece)],
+                    inbox.at[pl.ds(inbox_row(turn), piece)],
+                    send_sem,
+                    recv_sem.at[jnp.minimum(turn, 1)],
+                    peer,
+                ).start()
+                return 0
+
+            lax.fori_loop(jnp.where(column == 0, 1, 0), depth, send, 0)
+            return 0
+
+        lax.fori_loop(0, PLANE_XY, send_column, 0)
+        own_copy(turn).start()
         return 0
 
-    lax.fori_loop(0, states, one_state, 0)
-    for state in range(states):
-        pltpu.make_async_copy(
-            outbox.at[pl.ds((state * devices + me) * piece, piece)],
-            inbox.at[pl.ds((me * states + state) * piece, piece)],
-            own_sem.at[state],
-        ).wait()
-    wait_bytes(inbox.at[pl.ds(0, (devices - 1) * states * piece)], recv_sem)
-    wait_bytes(outbox.at[pl.ds(0, (devices - 1) * states * piece)], send_sem)
+    def inbox_row(turn):
+        owner = jnp.where(turn == 2, at_level(-toward) + mine, me)
+        return (owner * states + jnp.minimum(turn, 1)) * piece
+
+    def own_copy(turn):
+        return pltpu.make_async_copy(
+            outbox.at[pl.ds((turn * devices + me) * piece, piece)],
+            inbox.at[pl.ds(inbox_row(turn), piece)],
+            own_sem.at[turn],
+        )
+
+    lax.fori_loop(0, states + 1, one_turn, 0)
+    for turn in range(states + 1):
+        own_copy(turn).wait()
+    wait_bytes(inbox.at[pl.ds(0, (devices - 1) * piece)], recv_sem.at[0])
+    wait_bytes(inbox.at[pl.ds(0, (devices - 2) * piece)], recv_sem.at[1])
+    wait_bytes(outbox.at[pl.ds(0, (2 * devices - 3) * piece)], send_sem)
 
     total = devices * states
 
@@ -264,7 +296,6 @@
     rows_copy.start()
     half = total // 2
 
-    mine, level = lax.rem(me, PLANE_XY), lax.div(me, PLANE_XY)
 
     def part_of(ref, number):
         count = ref.shape[0] // PLANE_XY
@@ -382,8 +413,8 @@
             pltpu.VMEM(potential.shape, potential.dtype),
             pltpu.VMEM((2, planes + 4, width // 8, 8, GY), jnp.float32),
             pltpu.VMEM((planes, width // 8, 8, GY), jnp.float32),
-            pltpu.VMEM((GROUP, width, GY), jnp.float32),
-            pltpu.VMEM((count * planes * width, GY), jnp.float32),
+            pltpu.VMEM((count + 1, planes, width, GY), jnp.float32),
+            pltpu.VMEM(((count + 1) * planes * width, GY), jnp.float32),
             pltpu.VMEM((count * planes * width, GY), jnp.float32),
             pltpu.VMEM((total, points), jnp.float32),
             pltpu.VMEM((half, GY), jnp.float32),
@@ -395,12 +426,13 @@
             pltpu.VMEM((half, GY), jnp.float32),
             pltpu.VMEM((total, GY), jnp.float32),
             pltpu.SemaphoreType.DMA,
-            pltpu.SemaphoreType.DMA,
-            pltpu.SemaphoreType.DMA((count,)),
+            pltpu.SemaphoreType.DMA((2,)),
+            pltpu.SemaphoreType.DMA((count + 1,)),
             pltpu.SemaphoreType.DMA,
             pltpu.SemaphoreType.DMA((2, 3)),
             pltpu.SemaphoreType.DMA((2, 3)),
             pltpu.SemaphoreType.DMA((count + 1,)),
+            pltpu.SemaphoreType.DMA((2,)),
             pltpu.SemaphoreType.REGULAR,
             pltpu.SemaphoreType.REGULAR,
         ],

time: 87.3 us -> 83.2 us (0.953)
  Pallas kernels: 86.9 us -> 83 us
    pallas_call x1, Pallas kernels: 78.6 us -> 74.7 us  [filter_and_gram(): pl.pallas_call(filter_gram_kernel, out_shape=[jax.ShapeDtypeStruct((total...]
where the time goes in v5:
time: 83.2 us; the launch traced here: 83 us
  Pallas kernels  83 us (100%)
    pallas_call x1, Pallas kernels, filter_and_gram(): pl.pallas_call(filter_gram_kernel, out_shape=[jax.ShapeDtypeStruct((total...  74.7 us
    pallas_call x1, Pallas kernels, solve(): pl.pallas_call(functools.partial(solve_kernel, scale=scale), out_shape=ja...  8.32 us

profile of v5, /device:TPU:8, one launch (start us, length us, event | category | flops | bytes accessed | tf_op | source)
XLA Modules:
  0.0 83.0 jit_solution(7673118180635584033)
XLA Ops:
  0.0 74.7 %filter_and_gram.1 = (f32[256,1536]{1,0:T(8,128)}, f32[128,128]{1,0:T(8,128)}, f32[128,128]{1,0:T(8,128)}, f32[128,128]{1,0:T(8,128)}) custom-call(s32[2]{0:T(128)} %bounds_ref.1, bf16[2,32,48,128]{3,2,1,0:T(8,128)(2,1)} %states_ref.1, f32[32,48,128]{2,1,0:T(8,128)} %potential_ref.1), custom_call_target="tpu_custom_call" | custom-call | tf_op jit(solution)/shard_map/filter_and_gram/pallas_call | solution.py:397
  74.7 8.3 %solve.1 = f32[256,1536]{1,0:T(8,128)} custom-call(f32[128,128]{1,0:T(8,128)} %get-tuple-element.9.first_ref, f32[128,128]{1,0:T(8,128)} %get-tuple-element.10.low_ref, f32[128,128]{1,0:T(8,128)} %get-tuple-element.11.rest_ref, f32[256,1536]{1,0:T(8,128)} %get-tuple-element.12.rows_ref), custom_call_target="tpu_custom_call" | custom-call | tf_op jit(solution)/shard_map/solve/pallas_call | solution.py:541

commit v6 on v5

--- a/solution.py
+++ b/solution.py
@@ -27,15 +27,15 @@
 
 
 def circulant():
-    row = lax.rem(lax.broadcasted_iota(jnp.int32, (2 * GY, GY), 0), GY)
+    row = lax.broadcasted_iota(jnp.int32, (2 * GY, GY), 0)
     column = lax.broadcasted_iota(jnp.int32, (2 * GY, GY), 1)
-    apart = lax.rem(row - column + GY, GY)
+    apart = jnp.bitwise_and(row - column, GY - 1)
     near = jnp.where((apart == 1) | (apart == GY - 1), -16.0, 0.0)
     far = jnp.where((apart == 2) | (apart == GY - 2), 1.0, 0.0)
     return (near + far).astype(jnp.bfloat16)
 
 
-def filter_step(source, target, diagonal, matrix, factor, scale):
+def filter_step(source, target, diagonal, matrix, factor, finish=None):
     planes, rows = diagonal.shape[0], diagonal.shape[1]
     values = source[pl.ds(2, planes)].reshape(planes * rows * 8, GY)
     high = values.astype(jnp.bfloat16)
@@ -55,12 +55,13 @@
             far = (source[z, r] + source[z + 4, r]) + (ring[r] + ring[r + 4])
             total = far - 16.0 * near + diagonal[z, r] * here[r] + along_y[z, r]
             latest = factor * total - target[z + 2, r]
-            if scale is not None:
-                latest = latest * scale
-            target[z + 2, r] = latest
-
-
-GROUP = 4
+            if finish is None:
+                target[z + 2, r] = latest
+            else:
+                finish(z, r, latest)
+
+
+GROUP = 8
 PLANES_Z = 8
 PLANE_XY = 16
 
@@ -138,14 +139,21 @@
     piece = planes * width // devices
     me = lax.axis_index("state")
 
-    loads = [
-        pltpu.make_async_copy(potential_ref, potential, load_sem.at[states]),
-    ] + [
-        pltpu.make_async_copy(states_ref.at[state], initial.at[state], load_sem.at[state])
-        for state in range(states)
-    ]
-    for load in loads:
-        load.start()
+    pieces = planes // GROUP
+    loads = []
+    for number, (source, target) in enumerate(
+        [(potential_ref, potential)]
+        + [(states_ref.at[state], initial.at[state]) for state in range(states)]
+    ):
+        here = [pl.ds(piece * GROUP, GROUP) for piece in range(pieces)]
+        loads.append(
+            [
+                pltpu.make_async_copy(source.at[here[i]], target.at[here[i]], load_sem.at[number, i])
+                for i in range(pieces)
+            ]
+        )
+        for load in loads[number]:
+            load.start()
 
     barrier = pltpu.get_barrier_semaphore()
     greet(barrier, me, 16, 8)
@@ -167,10 +175,11 @@
     for buffer in range(2):
         for z in (0, 1, planes + 2, planes + 3):
             buffers[buffer, z] = zero
-    loads[0].wait()
-    lax.fori_loop(0, planes // GROUP, load_potential, 0)
     even, odd = buffers.at[0], buffers.at[1]
     matrix = circulant()
+    for load in loads[0]:
+        load.wait()
+    lax.fori_loop(0, planes // GROUP, load_potential, 0)
     toward = jnp.where(lax.axis_index("cuts") == 0, 1, -1)
     mine, level = lax.rem(me, PLANE_XY), lax.div(me, PLANE_XY)
 
@@ -187,7 +196,8 @@
         lax.fori_loop(0, planes // GROUP, convert, 0)
 
     lend = remote(start.at[1], start.at[2], lend_sem.at[0], lend_sem.at[1], at_level(toward) + mine)
-    loads[1].wait()
+    for load in loads[1]:
+        load.wait()
     to_float(0)
 
     def one_turn(turn, _):
@@ -207,35 +217,32 @@
 
         def two_steps(pair, _):
             first = jnp.where(pair == 0, 0.5 * factor, factor)
-            filter_step(even, odd, diagonal, matrix, first, None)
-
-            @pl.when((turn == 0) & (pair == 1))
+            filter_step(even, odd, diagonal, matrix, first)
+
+            @pl.when((turn == 0) & (pair == 0))
             def _():
                 pl.semaphore_wait(barrier, 7 + 3 + 3)
                 greet(heard_x, me, 1, 4)
-                loads[2].wait()
+                for load in loads[2]:
+                    load.wait()
                 to_float(1)
                 lend.start()
 
-            @pl.when((turn == 0) & (pair == 4))
+            @pl.when((turn == 0) & (pair == 3))
             def _():
                 pl.semaphore_wait(heard_x, 3)
                 greet(heard_y, me, 4, 4)
 
-            last = jnp.where(pair == DEGREE // 2 - 1, last_scale, 1.0)
-            filter_step(odd, even, diagonal, matrix, factor, last)
-            return 0
-
-        lax.fori_loop(0, DEGREE // 2, two_steps, 0)
-
-        def store(group, _):
-            for part in range(GROUP):
-                z = group * GROUP + part
-                for r in range(rows):
-                    outbox[pl.ds((turn * planes + z) * width + r, 8, stride=rows), :] = even[z + 2, r]
-            return 0
-
-        lax.fori_loop(0, planes // GROUP, store, 0)
+            filter_step(odd, even, diagonal, matrix, factor)
+            return 0
+
+        lax.fori_loop(0, DEGREE // 2 - 1, two_steps, 0)
+        filter_step(even, odd, diagonal, matrix, factor)
+
+        def finish(z, r, latest):
+            outbox[pl.ds((turn * planes + z) * width + r, 8, stride=rows), :] = latest * last_scale
+
+        filter_step(odd, even, diagonal, matrix, factor, finish)
 
         @pl.when(turn == 0)
         def _():
@@ -431,7 +438,7 @@
             pltpu.SemaphoreType.DMA,
             pltpu.SemaphoreType.DMA((2, 3)),
             pltpu.SemaphoreType.DMA((2, 3)),
-            pltpu.SemaphoreType.DMA((count + 1,)),
+            pltpu.SemaphoreType.DMA((count + 1, planes // GROUP)),
             pltpu.SemaphoreType.DMA((2,)),
             pltpu.SemaphoreType.REGULAR,
             pltpu.SemaphoreType.REGULAR,
@@ -501,15 +508,19 @@
 ):
     half = first_ref.shape[0]
     width = rows_ref.shape[1]
-    load = pltpu.make_async_copy(rows_ref, rows, rows_sem)
-    load.start()
+    loads = []
+    for number in range(rows_sem.shape[0]):
+        here = pl.ds(number * width // rows_sem.shape[0], width // rows_sem.shape[0])
+        loads.append(pltpu.make_async_copy(rows_ref.at[:, here], rows.at[:, here], rows_sem.at[number]))
+        loads[number].start()
     first_piece = 16 - width // 128
+    per_load = width // 128 // len(loads)
 
     def beside(tile):
         if tile < first_piece:
             return
-        if tile == first_piece:
-            load.wait()
+        if (tile - first_piece) % per_load == 0:
+            loads[(tile - first_piece) // per_load].wait()
         here = pl.ds((tile - first_piece) * 128, 128)
         upper = times(first_ref[...], rows[0:half, here], 1, 0)
         out[0:half, here] = upper * scale
@@ -547,7 +558,7 @@
             pltpu.VMEM((half, half), jnp.float32),
             pltpu.VMEM(rows.shape, jnp.float32),
             pltpu.VMEM(rows.shape, jnp.float32),
-            pltpu.SemaphoreType.DMA,
+            pltpu.SemaphoreType.DMA((4,)),
             pltpu.SemaphoreType.DMA((4,)),
         ],
         compiler_params=pltpu.CompilerParams(vmem_limit_bytes=56 << 20),

time: 83.2 us -> 82.1 us (0.987)
  Pallas kernels: 83 us -> 81.9 us
where the time goes in v6:
time: 82.1 us; the launch traced here: 81.9 us
  Pallas kernels  81.9 us (100%)
    pallas_call x1, Pallas kernels, filter_and_gram(): pl.pallas_call(filter_gram_kernel, out_shape=[jax.ShapeDtypeStruct((total...  74.3 us
    pallas_call x1, Pallas kernels, solve(): pl.pallas_call(functools.partial(solve_kernel, scale=scale), out_shape=ja...  7.67 us

profile of v6, /device:TPU:8, one launch (start us, length us, event | category | flops | bytes accessed | tf_op | source)
XLA Modules:
  0.0 81.9 jit_solution(15012470968505127200)
XLA Ops:
  0.0 74.3 %filter_and_gram.1 = (f32[256,1536]{1,0:T(8,128)}, f32[128,128]{1,0:T(8,128)}, f32[128,128]{1,0:T(8,128)}, f32[128,128]{1,0:T(8,128)}) custom-call(s32[2]{0:T(128)} %bounds_ref.1, bf16[2,32,48,128]{3,2,1,0:T(8,128)(2,1)} %states_ref.1, f32[32,48,128]{2,1,0:T(8,128)} %potential_ref.1), custom_call_target="tpu_custom_call" | custom-call | tf_op jit(solution)/shard_map/filter_and_gram/pallas_call | solution.py:404
  74.3 7.7 %solve.1 = f32[256,1536]{1,0:T(8,128)} custom-call(f32[128,128]{1,0:T(8,128)} %get-tuple-element.9.first_ref, f32[128,128]{1,0:T(8,128)} %get-tuple-element.10.low_ref, f32[128,128]{1,0:T(8,128)} %get-tuple-element.11.rest_ref, f32[256,1536]{1,0:T(8,128)} %get-tuple-element.12.rows_ref), custom_call_target="tpu_custom_call" | custom-call | tf_op jit(solution)/shard_map/solve/pallas_call | solution.py:552

commit v7 on v6

--- a/solution.py
+++ b/solution.py
@@ -177,9 +177,9 @@
             buffers[buffer, z] = zero
     even, odd = buffers.at[0], buffers.at[1]
     matrix = circulant()
-    for load in loads[0]:
-        load.wait()
-    lax.fori_loop(0, planes // GROUP, load_potential, 0)
+    for piece_number in range(pieces):
+        loads[0][piece_number].wait()
+        load_potential(piece_number, 0)
     toward = jnp.where(lax.axis_index("cuts") == 0, 1, -1)
     mine, level = lax.rem(me, PLANE_XY), lax.div(me, PLANE_XY)
 
@@ -252,10 +252,12 @@
         heading = jnp.where(turn == 1, -toward, toward)
         y, x = lax.div(mine, 4), lax.rem(mine, 4)
 
-        def send_column(column, _):
+        def send_column(count, _):
+            column = PLANE_XY - 1 - count
             beside = lax.rem(y + lax.div(column, 4), 4) * 4 + lax.rem(x + lax.rem(column, 4), 4)
 
-            def send(number, _):
+            def send(count, _):
+                number = depth - 1 - count
                 peer = at_level(number * heading) + beside
                 remote(
                     outbox.at[pl.ds((turn * devices + peer) * piece, piece)],
@@ -266,7 +268,7 @@
                 ).start()
                 return 0
 
-            lax.fori_loop(jnp.where(column == 0, 1, 0), depth, send, 0)
+            lax.fori_loop(0, jnp.where(column == 0, depth - 1, depth), send, 0)
             return 0
 
         lax.fori_loop(0, PLANE_XY, send_column, 0)
@@ -289,7 +291,6 @@
         own_copy(turn).wait()
     wait_bytes(inbox.at[pl.ds(0, (devices - 1) * piece)], recv_sem.at[0])
     wait_bytes(inbox.at[pl.ds(0, (devices - 2) * piece)], recv_sem.at[1])
-    wait_bytes(outbox.at[pl.ds(0, (2 * devices - 3) * piece)], send_sem)
 
     total = devices * states
 
@@ -395,6 +396,7 @@
         wait_bytes(in_column[which].at[pl.ds(0, PLANES_Z - 1)], sum_send.at[which, 1])
         wait_bytes(most_of(gathered[which]), sum_send.at[which, 2])
     rows_copy.wait()
+    wait_bytes(outbox.at[pl.ds(0, (2 * devices - 3) * piece)], send_sem)
 
 
 def filter_and_gram(states, potential, bounds):
@@ -486,10 +488,10 @@
             here = jnp.where(lane == start + i, jnp.where(row == i, 1.0, 0.0), here)
             pivot_row = of_row(here, i)
             solved = jnp.where(row == i, pivot_row * lax.rsqrt(pivot), solved)
-            others = jnp.where(row == i, 0.0, columns[i]) * inverses[i]
-            here = here - others * pivot_row
+            others = jnp.where(row == i, 0.0, columns[i])
+            here = here - (others * pivot_row) * inverses[i]
             for c in range(i + 1, 8):
-                columns[c] = columns[c] - others * of_row(columns[c], i)
+                columns[c] = columns[c] - (others * of_row(columns[c], i)) * inverses[i]
         result.append(jnp.where(lane <= start + row, solved, 0.0))
         spread = [of_row(here, c) * inverses[c] for c in range(8)]
         for multiplier, i in zip(multipliers, below):

time: 82.1 us -> 81.1 us (0.988)
  Pallas kernels: 81.9 us -> 80.5 us
    pallas_call x1, Pallas kernels: 74.3 us -> 72.9 us  [filter_and_gram(): pl.pallas_call(filter_gram_kernel, out_shape=[jax.ShapeDtypeStruct((total...]
where the time goes in v7:
time: 81.1 us; the launch traced here: 80.5 us
  Pallas kernels  80.5 us (99%)
    pallas_call x1, Pallas kernels, filter_and_gram(): pl.pallas_call(filter_gram_kernel, out_shape=[jax.ShapeDtypeStruct((total...  72.9 us
    pallas_call x1, Pallas kernels, solve(): pl.pallas_call(functools.partial(solve_kernel, scale=scale), out_shape=ja...  7.66 us

profile of v7, /device:TPU:8, one launch (start us, length us, event | category | flops | bytes accessed | tf_op | source)
XLA Modules:
  0.0 80.5 jit_solution(16985187138706143366)
XLA Ops:
  0.0 72.9 %filter_and_gram.1 = (f32[256,1536]{1,0:T(8,128)}, f32[128,128]{1,0:T(8,128)}, f32[128,128]{1,0:T(8,128)}, f32[128,128]{1,0:T(8,128)}) custom-call(s32[2]{0:T(128)} %bounds_ref.1, bf16[2,32,48,128]{3,2,1,0:T(8,128)(2,1)} %states_ref.1, f32[32,48,128]{2,1,0:T(8,128)} %potential_ref.1), custom_call_target="tpu_custom_call" | custom-call | tf_op jit(solution)/shard_map/filter_and_gram/pallas_call | solution.py:406
  72.9 7.7 %solve.1 = f32[256,1536]{1,0:T(8,128)} custom-call(f32[128,128]{1,0:T(8,128)} %get-tuple-element.9.first_ref, f32[128,128]{1,0:T(8,128)} %get-tuple-element.10.low_ref, f32[128,128]{1,0:T(8,128)} %get-tuple-element.11.rest_ref, f32[256,1536]{1,0:T(8,128)} %get-tuple-element.12.rows_ref), custom_call_target="tpu_custom_call" | custom-call | tf_op jit(solution)/shard_map/solve/pallas_call | solution.py:554

commit v8 on v7

--- a/solution.py
+++ b/solution.py
@@ -152,6 +152,8 @@
                 for i in range(pieces)
             ]
         )
+
+    for number in (2, 0, 1):
         for load in loads[number]:
             load.start()
 
@@ -177,9 +179,6 @@
             buffers[buffer, z] = zero
     even, odd = buffers.at[0], buffers.at[1]
     matrix = circulant()
-    for piece_number in range(pieces):
-        loads[0][piece_number].wait()
-        load_potential(piece_number, 0)
     toward = jnp.where(lax.axis_index("cuts") == 0, 1, -1)
     mine, level = lax.rem(me, PLANE_XY), lax.div(me, PLANE_XY)
 
@@ -196,6 +195,16 @@
         lax.fori_loop(0, planes // GROUP, convert, 0)
 
     lend = remote(start.at[1], start.at[2], lend_sem.at[0], lend_sem.at[1], at_level(toward) + mine)
+    for load in loads[2]:
+        load.wait()
+    to_float(1)
+    pl.semaphore_wait(barrier, 7 + 3 + 3)
+    lend.start()
+    greet(heard_x, me, 1, 4)
+
+    for piece_number in range(pieces):
+        loads[0][piece_number].wait()
+        load_potential(piece_number, 0)
     for load in loads[1]:
         load.wait()
     to_float(0)
@@ -218,15 +227,6 @@
         def two_steps(pair, _):
             first = jnp.where(pair == 0, 0.5 * factor, factor)
             filter_step(even, odd, diagonal, matrix, first)
-
-            @pl.when((turn == 0) & (pair == 0))
-            def _():
-                pl.semaphore_wait(barrier, 7 + 3 + 3)
-                greet(heard_x, me, 1, 4)
-                for load in loads[2]:
-                    load.wait()
-                to_float(1)
-                lend.start()
 
             @pl.when((turn == 0) & (pair == 3))
             def _():

time: 81.1 us -> 80.9 us (level)
  no operation moved by 1% of the time
where the time goes in v8:
time: 80.9 us; the launch traced here: 80.7 us
  Pallas kernels  80.7 us (100%)
    pallas_call x1, Pallas kernels, filter_and_gram(): pl.pallas_call(filter_gram_kernel, out_shape=[jax.ShapeDtypeStruct((total...  73 us
    pallas_call x1, Pallas kernels, solve(): pl.pallas_call(functools.partial(solve_kernel, scale=scale), out_shape=ja...  7.66 us

profile of v8, /device:TPU:8, one launch (start us, length us, event | category | flops | bytes accessed | tf_op | source)
XLA Modules:
  0.0 80.7 jit_solution(16568768226860116452)
XLA Ops:
  0.0 73.0 %filter_and_gram.1 = (f32[256,1536]{1,0:T(8,128)}, f32[128,128]{1,0:T(8,128)}, f32[128,128]{1,0:T(8,128)}, f32[128,128]{1,0:T(8,128)}) custom-call(s32[2]{0:T(128)} %bounds_ref.1, bf16[2,32,48,128]{3,2,1,0:T(8,128)(2,1)} %states_ref.1, f32[32,48,128]{2,1,0:T(8,128)} %potential_ref.1), custom_call_target="tpu_custom_call" | custom-call | tf_op jit(solution)/shard_map/filter_and_gram/pallas_call | solution.py:406
  73.0 7.7 %solve.1 = f32[256,1536]{1,0:T(8,128)} custom-call(f32[128,128]{1,0:T(8,128)} %get-tuple-element.9.first_ref, f32[128,128]{1,0:T(8,128)} %get-tuple-element.10.low_ref, f32[128,128]{1,0:T(8,128)} %get-tuple-element.11.rest_ref, f32[256,1536]{1,0:T(8,128)} %get-tuple-element.12.rows_ref), custom_call_target="tpu_custom_call" | custom-call | tf_op jit(solution)/shard_map/solve/pallas_call | solution.py:554
